TPU v7x, 128 devices: a whole 4x4x4 slice. The times are simulated.
128 devices in a mesh: batch: 128 (over z, x, y, core).
Axes of the slice: x: 4, y: 4, z: 4, core: 2. Of those that a mesh axis runs over, the one named last changes fastest.
Arguments:
- inputs: bfloat16 [384, 70, 1150], P('batch')
- d_out: bfloat16 [384, 70, 1150], P('batch'), may hold values from -6 to 6
- h_start: float32 [384, 1150], P('batch'), may hold values from -0.9 to 0.9
- c_start: float32 [384, 1150], P('batch'), may hold values from -4 to 4
- pieces: int32 [384, 3], P('batch'), may hold values from 1 to 40, 70 in all within a row
- in_mask: int32 [384, 1150], P('batch'), may hold values 0 or 1
- out_mask: int32 [384, 1150], P('batch'), may hold values 0 or 1
- w_mask: int32 [10584704], P('batch'), may hold values 0 or 1
- master: float32 [10584704], P('batch'), may hold values from -2 to 6
- moment_one: float32 [10584704], P('batch'), may hold values from -0.00048828125 to 0.00048828125
- moment_two: float32 [10584704], P('batch'), may hold values from 9.4476885e-11 to 3.7790754e-10
Outputs:
- output: bfloat16 [384, 70, 1150], P('batch')
- d_inputs: bfloat16 [384, 70, 1150], P('batch')
- moment_new: float32 [10584704], P('batch')
- second_new: float32 [10584704], P('batch')
- master_new: float32 [10584704], P('batch')
- grad_norm: float32 [], replicated
Inputs may be any that keep to these rules, and one draw needn't show every extreme that they name: `pieces`: each row's three lengths sum to 70; the padding comes last.
All inputs are finite; a program needn't handle non-finite values. No bound on the sum of `in_mask` or of `out_mask` or of `w_mask` on one device may be relied on, other than what follows from the above.
Results may differ from a plain program's by a relative error of at most 0.012.
The roundings to bfloat16 on the way count: a program that leaves them out, or rounds other values in their place, can miss the bound.
Values may be sent and summed in bfloat16 or wider, within the bound.
No kernel may reach another device: no remote copies, remote signals or barrier semaphores. Data moves between devices by JAX's collectives and lax.ppermute only.
A program may use at most 256 MiB of HBM per device.

v0:
```python
import jax
import jax.numpy as jnp
from jax import lax
from jax.sharding import PartitionSpec as P

STEP = 10


LEARN_RATE = 0.03
BETA_ONE = 0.9
BETA_TWO = 0.999
WEIGHT_DECAY = 0.01
EPSILON = 1e-08
CLIP_NORM = 1.0
KEEP_INPUT = 4.0 / 3.0
KEEP_OUTPUT = 4.0 / 3.0
KEEP_RECURRENT = 2.0


def unpack(full, width):
    gates_n = 4 * width
    count_w = 2 * width * gates_n
    weights = full[:count_w].reshape(width, 2 * gates_n)
    bias = full[count_w : count_w + gates_n].astype(jnp.float32)
    return (weights[:, :gates_n], weights[:, gates_n:], bias)


def right_product(left, matrix):
    return lax.dot_general(
        left, matrix, (((1,), (1,)), ((), ())), preferred_element_type=jnp.float32
    )


def left_product(left, right):
    return lax.dot_general(
        left, right, (((0,), (0,)), ((), ())), preferred_element_type=jnp.float32
    )


def body(
    inputs,
    d_out,
    h_start,
    c_start,
    pieces,
    in_mask,
    out_mask,
    w_mask,
    master,
    moment_one,
    moment_two,
):
    streams, steps, width = inputs.shape
    gates_n = 4 * width
    count_w = 2 * width * gates_n
    shard = master.shape[0]
    devices = lax.axis_size("batch")
    places = lax.axis_index("batch") * shard + lax.iota(jnp.int32, shard)
    recurrent = (places < count_w) & (places % (2 * gates_n) >= gates_n)
    rec_scale = jnp.where(recurrent, w_mask.astype(jnp.float32) * KEEP_RECURRENT, 1.0)
    local_low = master.astype(jnp.bfloat16) * rec_scale.astype(jnp.bfloat16)
    full = lax.all_gather(local_low, "batch", axis=0, tiled=True)
    w_in, w_rec, bias = unpack(full, width)
    position = lax.iota(jnp.int32, steps)
    keeps = 1.0 - (position[None, :] == pieces[:, 0:1]).astype(jnp.float32).T
    valid = (position[None, :] < pieces[:, 0:1] + pieces[:, 1:2]).astype(jnp.float32).T
    in_scale = in_mask.astype(jnp.float32) * KEEP_INPUT
    out_scale = out_mask.astype(jnp.float32) * KEEP_OUTPUT
    mixed = (jnp.transpose(inputs, (1, 0, 2)).astype(jnp.float32) * in_scale[None]).astype(
        jnp.bfloat16
    )
    mixed_rows = mixed.reshape(steps * streams, width)
    pre = (
        jnp.dot(mixed_rows, w_in, preferred_element_type=jnp.float32).reshape(
            steps, streams, gates_n
        )
        + bias
    )

    def forward_step(carry, slab):
        hidden, cell = carry
        pre_t, keep_t = slab
        hidden = hidden * keep_t[:, None]
        cell = cell * keep_t[:, None]
        hidden_low = hidden.astype(jnp.bfloat16)
        gates = pre_t + jnp.dot(hidden_low, w_rec, preferred_element_type=jnp.float32)
        in_gate = jax.nn.sigmoid(gates[:, :width])
        forget = jax.nn.sigmoid(gates[:, width : 2 * width])
        candid = jnp.tanh(gates[:, 2 * width : 3 * width])
        out_gate = jax.nn.sigmoid(gates[:, 3 * width :])
        cell_new = forget * cell + in_gate * candid
        hidden_new = out_gate * jnp.tanh(cell_new)
        return (
            (hidden_new, cell_new),
            (hidden_low, cell, in_gate, forget, candid, out_gate, cell_new),
        )

    _, kept = lax.scan(forward_step, (h_start, c_start), (pre, keeps))
    hidden_ins, cell_ins, in_gates, forgets, candids, out_gates, cells = kept
    masking = valid[:, :, None] * out_scale[None]
    states = out_gates * jnp.tanh(cells) * masking
    output = jnp.transpose(states, (1, 0, 2)).astype(jnp.bfloat16)
    full_again = lax.all_gather(local_low, "batch", axis=0, tiled=True)
    w_in_back, w_rec_back, unused_bias = unpack(full_again, width)
    coming = jnp.transpose(d_out, (1, 0, 2)).astype(jnp.float32) * masking

    def backward_step(carry, slab):
        dh_next, dc_next = carry
        come_t, keep_t, cell_in, in_gate, forget, candid, out_gate, cell_t = slab
        grad_h = come_t + dh_next
        squash = jnp.tanh(cell_t)
        grad_c = dc_next + grad_h * out_gate * (1.0 - squash * squash)
        pieces_grad = [
            grad_c * candid * in_gate * (1.0 - in_gate),
            grad_c * cell_in * forget * (1.0 - forget),
            grad_c * in_gate * (1.0 - candid * candid),
            grad_h * squash * out_gate * (1.0 - out_gate),
        ]
        dgates = jnp.concatenate(pieces_grad, axis=1).astype(jnp.bfloat16)
        dh_prev = right_product(dgates, w_rec_back) * keep_t[:, None]
        dc_prev = grad_c * forget * keep_t[:, None]
        return ((dh_prev, dc_prev), dgates)

    zero_state = jnp.zeros((streams, width), jnp.float32)
    _, dgates = lax.scan(
        backward_step,
        (zero_state, zero_state),
        (coming, keeps, cell_ins, in_gates, forgets, candids, out_gates, cells),
        reverse=True,
    )
    gate_rows = dgates.reshape(steps * streams, gates_n)
    grad_in = left_product(mixed_rows, gate_rows)
    grad_rec = left_product(hidden_ins.reshape(steps * streams, width), gate_rows)
    grad_bias = jnp.sum(gate_rows.astype(jnp.float32), axis=0)
    d_source = right_product(gate_rows, w_in_back).reshape(steps, streams, width) * in_scale[None]
    d_inputs = jnp.transpose(d_source, (1, 0, 2)).astype(jnp.bfloat16)
    tail = shard * devices - count_w - gates_n
    grad_all = jnp.concatenate(
        [
            jnp.concatenate([grad_in, grad_rec], axis=1).reshape(-1),
            grad_bias,
            jnp.zeros((tail,), jnp.float32),
        ]
    )
    grad_shard = lax.psum_scatter(grad_all, "batch", scatter_dimension=0, tiled=True) * rec_scale
    squares = lax.psum(jnp.sum(grad_shard * grad_shard), "batch")
    grad_norm = jnp.sqrt(squares)
    factor = jnp.minimum(1.0, CLIP_NORM / (grad_norm + 1e-06))
    clipped = grad_shard * factor
    moment_new = BETA_ONE * moment_one + (1.0 - BETA_ONE) * clipped
    second_new = BETA_TWO * moment_two + (1.0 - BETA_TWO) * clipped * clipped
    first_hat = moment_new / (1.0 - BETA_ONE**STEP)
    second_hat = second_new / (1.0 - BETA_TWO**STEP)
    master_new = master - LEARN_RATE * (
        first_hat / (jnp.sqrt(second_hat) + EPSILON) + WEIGHT_DECAY * master
    )
    return (output, d_inputs, moment_new, second_new, master_new, grad_norm)


def solution(mesh):
    placed = (
        P("batch", None, None),
        P("batch", None, None),
        P("batch", None),
        P("batch", None),
        P("batch", None),
        P("batch", None),
        P("batch", None),
        P("batch"),
        P("batch"),
        P("batch"),
        P("batch"),
    )
    return jax.shard_map(
        body,
        mesh=mesh,
        in_specs=placed,
        out_specs=(
            P("batch", None, None),
            P("batch", None, None),
            P("batch"),
            P("batch"),
            P("batch"),
            P(),
        ),
        check_vma=False,
    )
```

profile of v0, /device:TPU:1, one launch (start us, length us, event | category | flops | bytes accessed | tf_op | source)
XLA Modules:
  0.0 2401.6 jit_solution(17351001141981152688)
XLA Ops:
  8.6 7.2 broadcast.44
  20.5 227.1 %all-reduce.5.cloned.1.call-done = bf16[10584704]{0:T(1024)(128)(2,1)} async-done(((bf16[10584704]{0:T(1024)(128)(2,1)}), bf16[10584704]{0:T(1024)(128)(2,1)}) %all-reduce.5.cloned.1.call-update) | async-done | bytes 21169424
  247.6 15.0 slice.44
  262.7 32.4 %reshape.139 = bf16[1150,9200]{1,0:T(8,128)(2,1)} reshape(bf16[10580000]{0:T(1024)(128)(2,1)} %slice.44) | data formatting | bytes 42320000 | tf_op jit(solution)/shard_map/reshape | solution.py:23
  295.1 12.4 slice.47
  313.7 569.3 %while.45 = (s32[]{:T(128)}, f32[3,1150]{1,0:T(4,128)S(1)}, f32[3,1150]{1,0:T(4,128)S(1)}, bf16[70,3,1150]{2,1,0:T(4,128)(2,1)}, f32[70,3,1150]{2,1,0:T(4,128)},...) while((s32[]{:T(128)}, f32[3,1150]{1,0:T(4,128)S(1)}, ...), condition=%wide.region_1.2_spmd, body=%wide.region_0.1_spmd.sunk | while | flops 31826252 | bytes 11100917 | solution.py:98
  885.7 683.1 %while.46 = (s32[]{:T(128)}, f32[3,1150]{1,0:T(4,128)S(1)}, f32[3,1150]{1,0:T(4,128)S(1)}, bf16[70,3,4600]{2,1,0:T(4,128)(2,1)S(1)}, f32[70,3,1150]{2,0,1:T(8,12...) while((s32[]{:T(128)}, f32[3,1150]{1,0:T(4,128)S(1)}, ...), condition=%wide.region_3.4_spmd.clone, body=%wide.region_2.3_spmd.clone.sunk | while | flops 31846952 | bytes 11040375 | solution.py:125
  898.4 6.8 convolution_multiply_fusion.2
  917.9 6.8 convolution_multiply_fusion.2
  937.4 6.8 convolution_multiply_fusion.2
  947.2 6.8 convolution_multiply_fusion.2
  966.7 6.8 convolution_multiply_fusion.2
  976.4 6.8 convolution_multiply_fusion.2
  996.0 6.8 convolution_multiply_fusion.2
  1005.7 6.8 convolution_multiply_fusion.2
  1570.0 8.8 convolution_bitcast_fusion.1
  1578.8 8.8 convolution_bitcast_fusion
  1587.6 28.3 %pad_maximum_fusion = f32[1150,9200]{0,1:T(8,128)} fusion(f32[1150,4600]{0,1:T(8,128)} %convolution_bitcast_fusion, f32[1150,4600]{0,1:T(8,128)} %convolution_bitcast_fusion.1), kind=kLoop, calls=%fused_computation.63 | loop fusion | flops 10580000 | bytes 84640000 | tf_op jit(solution)/shard_map/concatenate | solution.py:140
  1615.9 42.3 %copy.46 = f32[1150,9200]{1,0:T(8,128)} copy(f32[1150,9200]{0,1:T(8,128)} %pad_maximum_fusion) | data formatting | bytes 84640000 | tf_op jit(solution)/shard_map/concatenate | solution.py:140
  1658.3 39.9 %reshape.140 = f32[10580000]{0:T(1024)} reshape(f32[1150,9200]{1,0:T(8,128)} %copy.46) | data formatting | bytes 84640000 | tf_op jit(solution)/shard_map/reshape | solution.py:140
  1698.2 321.0 %concatenate.41 = f32[10584704]{0:T(1024)} concatenate(f32[10580000]{0:T(1024)} %reshape.140, f32[4600]{0:T(1024)S(1)} %convert_reduce_fusion, f32[104]{0:T(128)S(1)} %broadcast_in_dim.56), dimensions={0} | concatenate | bytes 84677632 | tf_op jit(solution)/shard_map/concatenate | solution.py:138
  2019.2 8.3 fusion.31
  2027.5 295.6 %all-reduce.7.cloned.1.call-done = f32[10584704]{0:T(1024)} async-done(((f32[10584704]{0:T(1024)}), f32[10584704]{0:T(1024)}) %all-reduce.7.cloned.1.call-update) | async-done | bytes 42338832
  2325.0 65.6 %psum.7 = f32[]{:T(128)} all-reduce(f32[]{:T(128)} %get-tuple-element.523), channel_id=1, replica_groups=mesh['batch'=128] {'batch'}, use_global_device_ids=true, to_apply=%region_7.8 | all-reduce | flops 1 | bytes 8 | tf_op jit(solution)/shard_map/psum | solution.py:146
  (1028 shorter events, 1212.1 us)
Async XLA Ops:
  7.2 240.5 %all-reduce.5.cloned.1.call-start = ((), (), s32[]{:S(2)}) async-start(), calls=%async_computation | async-start | bytes 42340352
  19.5 0.7 copy-start.13
  19.5 1.0 copy-start.11
  19.5 1.0 copy-start.12
  19.6 2303.5 %all-reduce.7.cloned.1.call-start = ((), (), s32[]{:S(2)}) async-start(), calls=%async_computation.1 | async-start | bytes 84680704
  262.7 46.4 %copy-start.8 = (bf16[3,70,1150]{2,1,0:T(8,128)(2,1)S(1)}, bf16[3,70,1150]{2,1,0:T(8,128)(2,1)}, u32[]{:S(2)}) copy-start(bf16[3,70,1150]{2,1,0:T(8,128)(2,1)} %param.15) | copy-start | bytes 1449004
  295.1 14.2 copy-start
  309.3 4.5 copy-start.1
  309.3 4.5 copy-start.2
  313.7 569.4 %copy-start.7 = (bf16[3,70,1150]{2,1,0:T(8,128)(2,1)S(1)}, bf16[3,70,1150]{2,1,0:T(8,128)(2,1)}, u32[]{:S(2)}) copy-start(bf16[3,70,1150]{2,1,0:T(8,128)(2,1)} %param.16) | copy-start | bytes 1449004
  883.1 1.7 copy-start.3
  883.1 2.0 copy-start.4
  1568.9 1.1 copy-start.9
  1570.0 8.8 copy-start.10
  2019.2 303.9 %copy-start.6 = (s32[82693]{0:T(1024)S(1)}, s32[82693]{0:T(1024)}, u32[]{:S(2)}) copy-start(s32[82693]{0:T(1024)} %param.22) | copy-start | bytes 992320
  2019.2 372.2 %copy-start.5 = (f32[82693]{0:T(1024)S(1)}, f32[82693]{0:T(1024)}, u32[]{:S(2)}) copy-start(f32[82693]{0:T(1024)} %param.23) | copy-start | bytes 992320
Sparse Core Ops, SparseCore 0:
  19.7 227.8 all-reduce.4
  2019.3 303.7 all-reduce.6
where the time goes:
time: 2450 us; the launch traced here: 2400 us
  matrix products  896 us (37%)
  local copies, waits for them, and re-layouts  637 us (26%)
  waiting for transfers between devices  523 us (21%)
  other arithmetic  258 us (11%)
  blocking collectives  65.6 us (3%)
    unnamed x4, waiting for transfers between devices  523 us
    dot_general x71, matrix products, right_product(): lax.dot_general(left, matrix, (((1,), (1,)), ((), ())), preferred_element...  487 us
    dot_general x70, matrix products, forward_step(): jnp.dot(hidden_low, w_rec, preferred_element_type=jnp.float32)  387 us
    concatenate x1, local copies, waits for them, and re-layouts, body(): jnp.concatenate([jnp.concatenate([grad_in, grad_rec], axis=1).reshape(-1)...  321 us
    dynamic_update_slice x140, other arithmetic, body(): _, kept = lax.scan(forward_step, (h_start, c_start), (pre, keeps))  98.5 us
    dynamic_slice x70, local copies, waits for them, and re-layouts, body(): _, kept = lax.scan(forward_step, (h_start, c_start), (pre, keeps))  74.3 us
    psum x1, blocking collectives, body(): squares = lax.psum(jnp.sum(grad_shard * grad_shard), 'batch')  65.6 us
    dynamic_slice x70, local copies, waits for them, and re-layouts, body(): lax.scan(backward_step, (zero_state, zero_state), (coming, keeps, cell_in...  64.1 us
  transfers between devices with their start and end apart: 2, of which 2 were waited for; matrix products, arithmetic and copies ran while one was open for 0% of the time, Pallas kernels for 0%

commit v1 on v0

v1 whole, which is shorter than its diff:
```python
import functools

import jax
import jax.numpy as jnp
from jax import lax
from jax.experimental import pallas as pl
from jax.experimental.pallas import tpu as pltpu
from jax.sharding import PartitionSpec as P

STEP = 10


LEARN_RATE = 0.03
BETA_ONE = 0.9
BETA_TWO = 0.999
WEIGHT_DECAY = 0.01
EPSILON = 1e-08
CLIP_NORM = 1.0
KEEP_INPUT = 4.0 / 3.0
KEEP_OUTPUT = 4.0 / 3.0
KEEP_RECURRENT = 2.0

LONGEST = 40
LANES = 8
TILE = 8
OWN = TILE + 1
VMEM_LIMIT = 60 * 2**20

f32 = jnp.float32
bf16 = jnp.bfloat16


def dot(left, right):
    return lax.dot_general(left, right, (((1,), (0,)), ((), ())), preferred_element_type=f32)


def one_hot(rows, columns, wanted):
    row = lax.broadcasted_iota(jnp.int32, (rows, columns), 0)
    column = lax.broadcasted_iota(jnp.int32, (rows, columns), 1)
    return wanted(row, column).astype(bf16)


def place_of(natural, devices):
    owner, rest = natural // OWN, natural % OWN
    return jnp.where(rest < TILE, owner * TILE + rest, devices * TILE + owner)


def load_weights(wall, extra, half, into, sems, width, devices):
    main = devices * TILE
    gates_n = 4 * width
    copies = [
        pltpu.make_async_copy(
            wall.at[:, pl.ds(half * gates_n, gates_n)], into.at[pl.ds(0, main), :], sems.at[0]
        )
    ]
    for gate in range(4):
        copies.append(
            pltpu.make_async_copy(
                extra.at[pl.ds((4 * half + gate) * devices, devices), :],
                into.at[pl.ds(main, devices), pl.ds(gate * width, width)],
                sems.at[1 + gate],
            )
        )
    return copies


def step_rows(step):
    return pl.ds(pl.multiple_of(step * LANES, LANES), LANES)


def forward_kernel(
    devices,
    wall,
    extra,
    mixed,
    spread,
    collect,
    h_first,
    c_first,
    out_scale,
    hidden_rows,
    output_rows,
    kept,
    w_in,
    w_rec,
    pre,
    hiddens,
    outs,
    sems_in,
    sems_rec,
):
    width = mixed.shape[1]
    gates_n = 4 * width
    copies_in = load_weights(wall, extra, 0, w_in, sems_in, width, devices)
    copies_rec = load_weights(wall, extra, 1, w_rec, sems_rec, width, devices)
    for copy in copies_in + copies_rec:
        copy.start()
    rows = dot(spread[...], mixed[...]).astype(bf16)
    for copy in copies_in:
        copy.wait()
    chunk = 512

    def pre_chunk(index, carry):
        columns = pl.ds(pl.multiple_of(index * chunk, chunk), chunk)
        pre[:, columns] = dot(rows, w_in[:, columns])
        return carry

    lax.fori_loop(0, gates_n // chunk, pre_chunk, 0)
    for copy in copies_rec:
        copy.wait()
    scale = out_scale[...]

    def step(index, carry):
        hidden, cell = carry
        at = step_rows(index)
        gates = pre[at, :] + dot(hidden.astype(bf16), w_rec[...])
        in_gate = jax.nn.sigmoid(gates[:, :width])
        forget = jax.nn.sigmoid(gates[:, width : 2 * width])
        candid = jnp.tanh(gates[:, 2 * width : 3 * width])
        out_gate = jax.nn.sigmoid(gates[:, 3 * width :])
        cell_new = forget * cell + in_gate * candid
        squash = jnp.tanh(cell_new)
        hidden_new = out_gate * squash
        hiddens[at, :] = hidden
        outs[at, :] = hidden_new * scale
        kept[0, at, :] = out_gate * (1.0 - squash * squash)
        kept[1, at, :] = candid * in_gate * (1.0 - in_gate)
        kept[2, at, :] = cell * forget * (1.0 - forget)
        kept[3, at, :] = in_gate * (1.0 - candid * candid)
        kept[4, at, :] = squash * out_gate * (1.0 - out_gate)
        kept[5, at, :] = forget
        return (hidden_new, cell_new)

    lax.fori_loop(0, LONGEST, step, (h_first[...], c_first[...]))
    hidden_rows[...] = dot(collect[...], hiddens[...].astype(bf16)).astype(bf16)
    output_rows[...] = dot(collect[...], outs[...].astype(bf16)).astype(bf16)


def backward_kernel(
    devices,
    wall,
    extra,
    coming,
    spread,
    collect,
    out_scale,
    kept,
    gate_rows,
    w_rec,
    w_turned,
    come,
    dgates,
    sems,
):
    width = coming.shape[1]
    copies = load_weights(wall, extra, 1, w_rec, sems, width, devices)
    for copy in copies:
        copy.start()
    come[...] = dot(spread[...], coming[...])
    for copy in copies:
        copy.wait()

    def turn(index, carry):
        columns = pl.ds(pl.multiple_of(index * 128, 128), 128)
        w_turned[columns, :] = w_rec[:, columns].T
        return carry

    lax.fori_loop(0, 4 * width // 128, turn, 0)
    scale = out_scale[...]

    def step(count, carry):
        dh_next, dc_next = carry
        at = step_rows(LONGEST - 1 - count)
        grad_h = come[at, :] * scale + dh_next
        grad_c = dc_next + grad_h * kept[0, at, :]
        grads = jnp.concatenate(
            [
                grad_c * kept[1, at, :],
                grad_c * kept[2, at, :],
                grad_c * kept[3, at, :],
                grad_h * kept[4, at, :],
            ],
            axis=1,
        )
        dgates[at, :] = grads
        return (dot(grads.astype(bf16), w_turned[...]), grad_c * kept[5, at, :])

    zero = jnp.zeros((LANES, width), f32)
    lax.fori_loop(0, LONGEST, step, (zero, zero))
    for gate in range(4):
        columns = pl.ds(gate * width, width)
        gate_rows[gate] = dot(collect[...], dgates[:, columns].astype(bf16)).astype(bf16)


def in_vmem():
    return pl.BlockSpec(memory_space=pltpu.VMEM)


def in_place():
    return pl.BlockSpec(memory_space=pl.ANY)


def run_forward(devices, wall, extra, mixed, spread, collect, h_first, c_first, out_scale):
    steps_rows, rows = spread.shape
    width = mixed.shape[1]
    return pl.pallas_call(
        functools.partial(forward_kernel, devices),
        out_shape=(
            jax.ShapeDtypeStruct((rows, width), bf16),
            jax.ShapeDtypeStruct((rows, width), bf16),
            jax.ShapeDtypeStruct((6, steps_rows, width), f32),
        ),
        in_specs=[in_place()] * 2 + [in_vmem()] * 6,
        out_specs=(in_vmem(),) * 3,
        scratch_shapes=[
            pltpu.VMEM((width, 4 * width), bf16),
            pltpu.VMEM((width, 4 * width), bf16),
            pltpu.VMEM((steps_rows, 4 * width), f32),
            pltpu.VMEM((steps_rows, width), f32),
            pltpu.VMEM((steps_rows, width), f32),
            pltpu.SemaphoreType.DMA((5,)),
            pltpu.SemaphoreType.DMA((5,)),
        ],
        compiler_params=pltpu.CompilerParams(vmem_limit_bytes=VMEM_LIMIT),
        cost_estimate=pl.CostEstimate(
            flops=60_000_000_000, bytes_accessed=30_000_000, transcendentals=2_000_000
        ),
        name="forward",
    )(wall, extra, mixed, spread, collect, h_first, c_first, out_scale)


def run_backward(devices, wall, extra, coming, spread, collect, out_scale, kept):
    steps_rows, rows = spread.shape
    width = coming.shape[1]
    return pl.pallas_call(
        functools.partial(backward_kernel, devices),
        out_shape=jax.ShapeDtypeStruct((4, rows, width), bf16),
        in_specs=[in_place()] * 2 + [in_vmem()] * 5,
        out_specs=in_vmem(),
        scratch_shapes=[
            pltpu.VMEM((width, 4 * width), bf16),
            pltpu.VMEM((4 * width, width), bf16),
            pltpu.VMEM((steps_rows, width), f32),
            pltpu.VMEM((steps_rows, 4 * width), f32),
            pltpu.SemaphoreType.DMA((5,)),
        ],
        compiler_params=pltpu.CompilerParams(vmem_limit_bytes=VMEM_LIMIT),
        cost_estimate=pl.CostEstimate(
            flops=60_000_000_000, bytes_accessed=30_000_000, transcendentals=0
        ),
        name="backward",
    )(wall, extra, coming, spread, collect, out_scale, kept)


def split_exact(values):
    parts = []
    rest = values
    for _ in range(3):
        part = lax.reduce_precision(rest, 8, 7)
        parts.append(part.astype(bf16))
        rest = rest - part
    return parts


def body(
    inputs,
    d_out,
    h_start,
    c_start,
    pieces,
    in_mask,
    out_mask,
    w_mask,
    master,
    moment_one,
    moment_two,
):
    streams, steps, width = inputs.shape
    gates_n = 4 * width
    count_w = 2 * width * gates_n
    total = count_w + gates_n
    shard = master.shape[0]
    devices = lax.axis_size("batch")
    me = lax.axis_index("batch")
    wide = OWN * devices
    block = OWN * 2 * gates_n
    gap = block - shard
    most = gap * devices
    tokens = streams * steps
    rows_n = -(-tokens // 32) * 32
    line = 8
    lines = devices // line

    line_groups = [[line * q + m for m in range(line)] for q in range(lines)]
    across_groups = [[line * q + m for q in range(lines)] for m in range(line)]
    column_groups = [
        [line * q + 2 * y + c for y in range(line // 2)] for q in range(lines) for c in range(2)
    ]
    twins = [(i, i ^ 1) for i in range(devices)]

    to_kept = one_hot(width, wide, lambda k, p: place_of(k, devices) == p)
    to_natural = one_hot(wide, width, lambda p, k: place_of(k, devices) == p)

    places = me * shard + lax.iota(jnp.int32, shard)
    recurrent = (places < count_w) & (places % (2 * gates_n) >= gates_n)
    rec_scale = jnp.where(recurrent, w_mask.astype(f32) * KEEP_RECURRENT, 1.0)
    local_low = master.astype(bf16) * rec_scale.astype(bf16)
    local_low = jnp.where(places < total, local_low, jnp.zeros((), bf16))
    head = lax.ppermute(local_low[:most], "batch", [(i + 1, i) for i in range(devices - 1)])
    own = lax.dynamic_slice(jnp.concatenate([local_low, head]), (gap * me,), (block,))
    own = own.reshape(OWN * 8, width)
    order = one_hot(
        OWN * 8,
        OWN * 8,
        lambda a, b: jnp.where(a < 64, (a % 8) * 8 + a // 8, 64 + a % 8) == b,
    )
    own = dot(order, dot(own, to_kept).astype(bf16)).astype(bf16)
    own = jnp.concatenate([own[TILE * j : TILE * (j + 1)] for j in range(OWN)], axis=1)
    wall = lax.all_gather(own, "batch", axis=0, tiled=True)
    gather_ninth = one_hot(
        8 * devices, 8 * devices, lambda a, b: (a % devices) * 8 + a // devices == b
    )
    extra = dot(gather_ninth, wall[:, 8 * wide :]).astype(bf16)

    in_scale = in_mask.astype(f32) * KEEP_INPUT
    mixed = (inputs.astype(f32) * in_scale[:, None, :]).astype(bf16).reshape(tokens, width)
    spare = ((0, rows_n - tokens), (0, 0))
    mixed = dot(jnp.pad(mixed, spare), to_kept).astype(bf16)
    bias_place = place_of(jnp.int32(width), devices)
    column = lax.broadcasted_iota(jnp.int32, mixed.shape, 1)
    mixed = jnp.where(column == bias_place, jnp.ones((), bf16), mixed)
    coming = dot(jnp.pad(d_out.reshape(tokens, width), spare), to_kept).astype(bf16)
    small = jnp.concatenate(
        [h_start.astype(bf16)]
        + split_exact(c_start)
        + [in_mask.astype(bf16), out_mask.astype(bf16)],
        axis=0,
    )
    small = dot(small, to_kept)
    part = [small[streams * j : streams * (j + 1)] for j in range(6)]
    empty = jnp.zeros((LANES - streams, wide), f32)
    h_first = jnp.concatenate([part[0], empty], axis=0)
    c_first = jnp.concatenate([part[1] + part[2] + part[3], empty], axis=0)
    in_scale_kept = part[4] * KEEP_INPUT
    out_scale_kept = part[5] * KEEP_OUTPUT
    out_scale = jnp.concatenate(
        [out_scale_kept, out_scale_kept, jnp.zeros((LANES - 2 * streams, wide), f32)], axis=0
    )
    base = jnp.arange(streams, dtype=jnp.int32) * steps
    none = jnp.zeros((LANES - 2 * streams,), jnp.int32)
    begins = jnp.concatenate([base, base + pieces[:, 0], none])
    lengths = jnp.concatenate([pieces[:, 0], pieces[:, 1], none])
    ticks = lax.broadcasted_iota(jnp.int32, (LONGEST, LANES), 0)
    where = jnp.where(ticks < lengths[None, :], begins[None, :] + ticks, -1).reshape(-1)
    spread = (where[:, None] == lax.iota(jnp.int32, rows_n)[None, :]).astype(bf16)
    collect = (lax.iota(jnp.int32, rows_n)[:, None] == where[None, :]).astype(bf16)

    hidden_rows, output_rows, kept = run_forward(
        devices, wall, extra, mixed, spread, collect, h_first, c_first, out_scale
    )

    core = me % 2
    mine = jnp.where(core == 0, mixed, hidden_rows)
    other = lax.ppermute(jnp.where(core == 0, hidden_rows, mixed), "batch", twins)
    left_mine = lax.all_gather(
        mine, "batch", axis=0, tiled=True, axis_index_groups=column_groups
    )
    left_other = lax.all_gather(
        other, "batch", axis=0, tiled=True, axis_index_groups=column_groups
    )

    gate_rows = run_backward(devices, wall, extra, coming, spread, collect, out_scale, kept)

    right_mine = lax.all_to_all(
        gate_rows, "batch", 0, 0, tiled=True, axis_index_groups=column_groups
    ).reshape(4 * rows_n, wide)
    right_other = lax.ppermute(right_mine, "batch", twins)

    def turned_dot(left, right):
        return lax.dot_general(left, right, (((0,), (0,)), ((), ())), preferred_element_type=f32)

    grad = turned_dot(left_mine, right_mine) + turned_dot(left_other, right_other)
    grad = grad.astype(bf16)
    main = devices * TILE
    grad = jnp.concatenate(
        [
            grad[:main].reshape(lines, line * TILE, wide),
            grad[main:].reshape(lines, line, wide),
        ],
        axis=1,
    )
    grad = lax.psum_scatter(
        grad, "batch", scatter_dimension=0, tiled=True, axis_index_groups=across_groups
    ).reshape(line * OWN, wide)

    slot = 16
    send = one_hot(
        line * slot,
        line * OWN,
        lambda a, b: ((a % slot < TILE) & (a // slot * TILE + a % slot == b))
        | ((a % slot == TILE) & (line * TILE + a // slot == b)),
    )
    home = lax.all_to_all(
        dot(send, grad).astype(bf16), "batch", 0, 0, tiled=True, axis_index_groups=line_groups
    )
    settle = one_hot(
        OWN * 8,
        line * slot,
        lambda a, b: (a % 4 * 2 + a // 4 % 2) * slot + a // 8 == b,
    )
    home = dot(dot(settle, home).astype(bf16), to_natural).astype(bf16).reshape(block)
    tail = lax.ppermute(home[block - most :], "batch", [(i, i + 1) for i in range(devices - 1)])
    grad_shard = lax.dynamic_slice(
        jnp.concatenate([tail, home]), (most - gap * me,), (shard,)
    ).astype(f32)
    grad_shard = grad_shard * rec_scale
    squares = jnp.broadcast_to(jnp.sum(grad_shard * grad_shard), (devices, 128))
    squares = jnp.sum(lax.all_to_all(squares, "batch", 0, 0, tiled=True)[:, 0])
    grad_norm = jnp.sqrt(squares)

    output = dot(output_rows, to_natural)[:tokens].astype(bf16).reshape(streams, steps, width)
    gates_flat = [gate_rows[gate] for gate in range(4)]
    d_main = sum(
        lax.dot_general(
            gates_flat[gate],
            wall[:, gate * wide : (gate + 1) * wide],
            (((1,), (1,)), ((), ())),
            preferred_element_type=f32,
        )
        for gate in range(4)
    )
    d_extra = sum(
        lax.dot_general(
            gates_flat[gate],
            extra[gate * devices : (gate + 1) * devices],
            (((1,), (1,)), ((), ())),
            preferred_element_type=f32,
        )
        for gate in range(4)
    )
    row_stream = lax.iota(jnp.int32, rows_n) // steps
    d_rows = jnp.concatenate([d_main, d_extra], axis=1)
    stream_scale = sum(
        jnp.where((row_stream == s)[:, None], in_scale_kept[s][None, :], 0.0)
        for s in range(streams)
    )
    d_rows = (d_rows * stream_scale).astype(bf16)
    d_inputs = dot(d_rows, to_natural)[:tokens].astype(bf16).reshape(streams, steps, width)

    factor = jnp.minimum(1.0, CLIP_NORM / (grad_norm + 1e-06))
    clipped = grad_shard * factor
    moment_new = BETA_ONE * moment_one + (1.0 - BETA_ONE) * clipped
    second_new = BETA_TWO * moment_two + (1.0 - BETA_TWO) * clipped * clipped
    first_hat = moment_new / (1.0 - BETA_ONE**STEP)
    second_hat = second_new / (1.0 - BETA_TWO**STEP)
    master_new = master - LEARN_RATE * (
        first_hat / (jnp.sqrt(second_hat) + EPSILON) + WEIGHT_DECAY * master
    )
    return (output, d_inputs, moment_new, second_new, master_new, grad_norm)


def solution(mesh):
    placed = (
        P("batch", None, None),
        P("batch", None, None),
        P("batch", None),
        P("batch", None),
        P("batch", None),
        P("batch", None),
        P("batch", None),
        P("batch"),
        P("batch"),
        P("batch"),
        P("batch"),
    )
    return jax.shard_map(
        body,
        mesh=mesh,
        in_specs=placed,
        out_specs=(
            P("batch", None, None),
            P("batch", None, None),
            P("batch"),
            P("batch"),
            P("batch"),
            P(),
        ),
        check_vma=False,
    )
```

time: 2450 us -> 455 us (0.19); the launches traced: 2400 us -> 454 us
  matrix products: 896 us -> 48.3 us
  local copies, waits for them, and re-layouts: 637 us -> 9.58 us
  waiting for transfers between devices: 523 us -> 182 us
  other arithmetic: 258 us -> 13.6 us
  Pallas kernels: 0 us -> 153 us
  blocking collectives: 65.6 us -> 0 us
  starting transfers between devices: 0.08 us -> 30.4 us
    dot_general x144 -> x19, matrix products: 896 us -> 48.3 us  [the longest x9 18.8 us: dot(): lax.dot_general(left, right, (((1,), (0,)), ((), ())), preferred_element_...]
    unnamed x4 -> x5, waiting for transfers between devices: 523 us -> 56.7 us
    concatenate x142 -> x4, local copies, waits for them, and re-layouts: 382 us -> 1.04 us  [the longest x1 0.62 us: body(): c_first = jnp.concatenate([part[1] + part[2] + part[3], empty], axis=0)]
    pallas_call x0 -> x2, Pallas kernels: none -> 153 us  [the longest x1 78.2 us: run_forward(): pl.pallas_call(functools.partial(forward_kernel, devices), out_shape=(jax...]
    dynamic_slice x140 -> x0, local copies, waits for them, and re-layouts: 138 us -> none  [the longest x70 74.3 us: body(): _, kept = lax.scan(forward_step, (h_start, c_start), (pre, keeps))]
    dynamic_update_slice x140 -> x0, other arithmetic: 98.5 us -> none  [body(): _, kept = lax.scan(forward_step, (h_start, c_start), (pre, keeps))]
    all_gather x0 -> x3, waiting for transfers between devices: none -> 83.5 us  [the longest x1 83.5 us: body(): wall = lax.all_gather(own, 'batch', axis=0, tiled=True)]
    reshape x2 -> x7, local copies, waits for them, and re-layouts: 72.3 us -> 3.01 us  [the longest x1 0.97 us: body(): dot(output_rows, to_natural)[:tokens].astype(bf16)]
  transfers between devices with their start and end apart: 2 -> 11, of which waited for: 2 -> 7; matrix products, arithmetic and copies ran while one was open for 0% -> 9% of each run, Pallas kernels for 0% -> 17%
where the time goes in v1:
time: 455 us; the launch traced here: 454 us
  waiting for transfers between devices  182 us (40%)
  Pallas kernels  153 us (34%)
  matrix products  48.3 us (11%)
  starting transfers between devices  30.4 us (7%)
  between operations  16.5 us (4%)
  other arithmetic  13.6 us (3%)
  local copies, waits for them, and re-layouts  9.58 us (2%)
    all_gather x1, waiting for transfers between devices, body(): wall = lax.all_gather(own, 'batch', axis=0, tiled=True)  83.5 us
    pallas_call x1, Pallas kernels, run_forward(): pl.pallas_call(functools.partial(forward_kernel, devices), out_shape=(jax...  78.2 us
    pallas_call x1, Pallas kernels, run_backward(): pl.pallas_call(functools.partial(backward_kernel, devices), out_shape=jax...  75.1 us
    unnamed x5, waiting for transfers between devices  56.7 us
    all_to_all x1, waiting for transfers between devices, body(): lax.all_to_all(gate_rows, 'batch', 0, 0, tiled=True, axis_index_groups=co...  30.8 us
    dot_general x9, matrix products, dot(): lax.dot_general(left, right, (((1,), (0,)), ((), ())), preferred_element_...  18.8 us
    dot_general x2, matrix products, turned_dot(): lax.dot_general(left, right, (((0,), (0,)), ((), ())), preferred_element_...  14 us
    dot_general x4, matrix products, body(): lax.dot_general(gates_flat[gate], wall[:, gate * wide:(gate + 1) * wide],...  10.4 us
  transfers between devices with their start and end apart: 11, of which 7 were waited for; matrix products, arithmetic and copies ran while one was open for 9% of the time, Pallas kernels for 17%

profile of v1, /device:TPU:1, one launch (start us, length us, event | category | flops | bytes accessed | tf_op | source)
XLA Modules:
  0.0 453.8 jit_solution(15443628001159800420)
XLA Ops:
  8.6 3.3 collective-permute-start
  12.5 1.9 fusion.2
  27.1 83.5 %all-gather.4.cloned.1.call-done.wall = bf16[1024,10368]{1,0:T(8,128)(2,1)} async-done(((bf16[8,10368]{1,0:T(8,128)(2,1)}), bf16[1024,10368]{1,0:T(8,128)(2,1)}) %all-gather.4.cloned.1.call-update) | async-done | bytes 21233680 | tf_op jit(solution)/shard_map/all_gather | solution.py:319
  110.6 6.5 %fusion.6.extra = bf16[1024,1152]{1,0:T(8,128)(2,1)} fusion(bf16[1024,10368]{1,0:T(8,128)(2,1)} %all-gather.4.cloned.1.call-done.wall, s32[1024]{0:T(1024)S(1)} %get-tuple-element.44, s32[1024]{0:T(1024)S(1)} %get-tuple-element.47, s32[1024]{0:T(1024)S(1)} %get-tuple-element.45, s32[1024]{0:T(1024)S(1)} %get-tuple-element.46, ...), kind=kOutput, calls=%fused_computation.16 | convolution fusion | flops 2422341632 | bytes 4737024 | tf_op jit(solution)/shard_map/dot_general | solution.py:34
  117.1 78.2 %forward.1 = (bf16[224,1152]{1,0:T(8,128)(2,1)}, bf16[224,1152]{1,0:T(8,128)(2,1)}, f32[6,320,1152]{2,1,0:T(8,128)}) custom-call(bf16[1024,10368]{1,0:T(8,128)(2,1)} %all-gather.4.cloned.1.call-done.wall, bf16[1024,1152]{1,0:T(8,128)(2,1)} %fusion.6.extra, bf16[224,1152]{1,0:T(8,128)(2,1)} %fusion.7.mixed, bf16[320,224]{1,0:T(8,128)(2,1)} %fusion.57.spread, ...), custom_call_target="tpu_custom_call" | custom-call | flops 60000002048 | bytes 30000000 | tf_op jit(solution)/shard_map/forward/pallas_call | solution.py:206
  195.3 2.0 broadcast_select_fusion
  197.3 75.1 %backward.1 = bf16[4,224,1152]{2,1,0:T(8,128)(2,1)} custom-call(bf16[1024,10368]{1,0:T(8,128)(2,1)} %all-gather.4.cloned.1.call-done.wall, bf16[1024,1152]{1,0:T(8,128)(2,1)} %fusion.6.extra, bf16[224,1152]{1,0:T(8,128)(2,1)} %convolution_convert_fusion.coming, bf16[320,224]{1,0:T(8,128)(2,1)} %fusion.57.spread, bf16[224,320]{1,0:T(8,128)(2,1)} %fusion.46.collect, ...), custom_call_target="tpu_custom_call" | custom-call | flops 60000002048 | bytes 30000000 | tf_op jit(solution)/shard_map/backward/pallas_call | solution.py:235
  272.4 4.0 all-to-all-start
  279.3 30.8 %all-to-all-done = bf16[4,224,1152]{2,1,0:T(8,128)(2,1)S(1)} async-done(((bf16[4,224,1152]{2,1,0:T(8,128)(2,1)}), bf16[4,224,1152]{2,1,0:T(8,128)(2,1)S(1)}, u32[]{:S(2)}, u32[]{:S(2)}) %all-to-all-start) | async-done | bytes 2064416 | tf_op jit(solution)/shard_map/all_to_all | solution.py:374
  310.1 3.4 collective-permute-start.2
  313.5 7.1 %fusion.168 = f32[1152,1152]{1,0:T(8,128)} fusion(bf16[896,1152]{1,0:T(8,128)(2,1)} %all-gather.6.cloned.1.call-done, bf16[896,1152]{1,0:T(8,128)(2,1)S(1)} %bitcast.41), kind=kOutput, calls=%fused_computation.260 | convolution fusion | flops 2378170368 | bytes 9437184 | tf_op jit(solution)/shard_map/dot_general | solution.py:380
  320.6 6.9 %fusion = bf16[1152,1152]{1,0:T(8,128)(2,1)S(1)} fusion(f32[1152,1152]{1,0:T(8,128)} %fusion.168, bf16[896,1152]{1,0:T(8,128)(2,1)} %all-gather.8.cloned.1.call-done, bf16[896,1152]{1,0:T(8,128)(2,1)} %collective-permute-done.2), kind=kOutput, calls=%fused_computation.9 | convolution fusion | flops 2380824576 | bytes 12091392 | tf_op jit(solution)/shard_map/dot_general | solution.py:380
  333.6 2.6 fusion.8
  336.2 2.6 fusion.10
  338.8 2.6 fusion.12
  341.4 2.6 fusion.30
  344.1 56.6 %reduce-scatter.4.cloned.1.call-done = bf16[1,72,1152]{2,1,0:T(8,128)(2,1)} async-done(((bf16[16,72,1152]{2,1,0:T(8,128)(2,1)}), bf16[1,72,1152]{2,1,0:T(8,128)(2,1)}) %reduce-scatter.4.cloned.1.call-update) | async-done | bytes 165904
  400.7 2.0 convolution_convert_fusion.2
  402.7 6.5 %all-to-all-start.1 = ((bf16[8,16,1152]{2,1,0:T(8,128)(2,1)}), bf16[8,16,1152]{2,1,0:T(8,128)(2,1)S(1)}, u32[]{:S(2)}, u32[]{:S(2)}) async-start(bf16[8,16,1152]{2,1,0:T(8,128)(2,1)} %bitcast.8), calls=%async_computation.1 | async-start | bytes 589824 | tf_op jit(solution)/shard_map/all_to_all | solution.py:403
  411.7 4.3 all-to-all-done.1
  417.7 3.4 collective-permute-start.3
  425.1 9.0 %all-to-all-start.2 = ((f32[128,1,128]{2,1,0:T(1,128)}), f32[128,1,128]{2,1,0:T(1,128)S(1)}, u32[]{:S(2)}, u32[]{:S(2)}) async-start(f32[128,1,128]{2,1,0:T(1,128)} %broadcast_in_dim.94), calls=%async_computation.2 | async-start | bytes 131072 | tf_op jit(solution)/shard_map/all_to_all | solution.py:418
  434.1 2.3 fusion.164
  438.4 5.2 %all-to-all-done.2 = f32[128,1,128]{2,1,0:T(1,128)S(1)} async-done(((f32[128,1,128]{2,1,0:T(1,128)}), f32[128,1,128]{2,1,0:T(1,128)S(1)}, u32[]{:S(2)}, u32[]{:S(2)}) %all-to-all-start.2) | async-done | bytes 65568 | tf_op jit(solution)/shard_map/all_to_all | solution.py:418
  (162 shorter events, 35.1 us)
Async XLA Ops:
  7.2 103.5 %all-gather.4.cloned.1.call-start = ((), (), s32[]{:S(2)}) async-start(), calls=%async_computation.4 | async-start | bytes 21399552 | tf_op jit(solution)/shard_map/all_gather | solution.py:319
  8.6 6.1 %collective-permute-start = (bf16[13696]{0:T(1024)(128)(2,1)S(1)}, bf16[13696]{0:T(1024)(128)(2,1)S(1)}, u32[]{:S(2)}, u32[]{:S(2)}) collective-permute-start(bf16[13696]{0:T(1024)(128)(2,1)S(1)} %slice.164), channel_id=1, source_target_pairs={{1,0},{2,1},{3,2},{4,3},{5,4},{6,5},{7,6},{8,7},{9,8},{10,9},{11,1... | collective-permute-start | bytes 82184 | tf_op jit(solution)/shard_map/ppermute | solution.py:309
  17.6 295.9 %all-gather.6.cloned.1.call-start = ((), (), s32[]{:S(2)}) async-start(), calls=%async_computation.5 | async-start | bytes 2580480 | tf_op jit(solution)/shard_map/all_gather | solution.py:365
  117.1 78.2 %copy-start.3 = (bf16[224,1152]{1,0:T(8,128)(2,1)S(1)}, bf16[224,1152]{1,0:T(8,128)(2,1)}, u32[]{:S(2)}) copy-start(bf16[224,1152]{1,0:T(8,128)(2,1)} %fusion.7.mixed) | copy-start | bytes 1548292
  272.4 37.7 %all-to-all-start = ((bf16[4,224,1152]{2,1,0:T(8,128)(2,1)}), bf16[4,224,1152]{2,1,0:T(8,128)(2,1)S(1)}, u32[]{:S(2)}, u32[]{:S(2)}) async-start(bf16[4,224,1152]{2,1,0:T(8,128)(2,1)} %backward.1), calls=%async_computation | async-start | bytes 4128768 | tf_op jit(solution)/shard_map/all_to_all | solution.py:374
  276.4 44.2 %all-gather.8.cloned.1.call-start = ((), (), s32[]{:S(2)}) async-start(), calls=%async_computation.6 | async-start | bytes 2580480 | tf_op jit(solution)/shard_map/all_gather | solution.py:368
  276.4 2.1 collective-permute-start.1
  279.3 121.4 %reduce-scatter.4.cloned.1.call-start = ((), (), s32[]{:S(2)}) async-start(), calls=%async_computation.7 | async-start | bytes 2820096
  310.1 10.5 %collective-permute-start.2 = (bf16[896,1152]{1,0:T(8,128)(2,1)S(1)}, bf16[896,1152]{1,0:T(8,128)(2,1)}, u32[]{:S(2)}, u32[]{:S(2)}) collective-permute-start(bf16[896,1152]{1,0:T(8,128)(2,1)S(1)} %bitcast.40), channel_id=1, source_target_pairs={{0,1},{1,0},{2,3},{3,2},{4,5},{5,4},{6,7},{7,6},{8,9},{9,8},{10,11... | collective-permute-start | bytes 6193160 | tf_op jit(solution)/shard_map/ppermute | solution.py:377
  344.0 72.0 %copy-start.12 = (s32[1150]{0:T(1024)S(1)}, s32[1150]{0:T(1024)}, u32[]{:S(2)}) copy-start(s32[1150]{0:T(1024)} %copy-done.11) | copy-start | bytes 13804
  344.0 72.0 %copy-start.14 = (s32[1150]{0:T(1024)S(1)}, s32[1150]{0:T(1024)}, u32[]{:S(2)}) copy-start(s32[1150]{0:T(1024)} %copy-done.13) | copy-start | bytes 13804
  344.0 72.0 %copy-start.16 = (s32[1150]{0:T(1024)S(1)}, s32[1150]{0:T(1024)}, u32[]{:S(2)}) copy-start(s32[1150]{0:T(1024)} %copy-done.15) | copy-start | bytes 13804
  344.0 72.0 %copy-start.18 = (s32[1150]{0:T(1024)S(1)}, s32[1150]{0:T(1024)}, u32[]{:S(2)}) copy-start(s32[1150]{0:T(1024)} %copy-done.17) | copy-start | bytes 13804
  344.0 72.0 %copy-start.23 = (pred[1150]{0:T(1024)(128)(4,1)S(1)}, pred[1150]{0:T(1024)(128)(4,1)}, u32[]{:S(2)}) copy-start(pred[1150]{0:T(1024)(128)(4,1)} %copy-done.22) | copy-start | bytes 3454
  344.0 72.0 %copy-start.25 = (pred[1150]{0:T(1024)(128)(4,1)S(1)}, pred[1150]{0:T(1024)(128)(4,1)}, u32[]{:S(2)}) copy-start(pred[1150]{0:T(1024)(128)(4,1)} %copy-done.24) | copy-start | bytes 3454
  344.0 72.0 %copy-start.29 = (s32[72]{0:T(128)S(1)}, s32[72]{0:T(128)}, u32[]{:S(2)}) copy-start(s32[72]{0:T(128)} %copy-done.28) | copy-start | bytes 868
  344.1 72.0 %copy-start.31 = (s32[72]{0:T(128)S(1)}, s32[72]{0:T(128)}, u32[]{:S(2)}) copy-start(s32[72]{0:T(128)} %copy-done.30) | copy-start | bytes 868
  344.1 72.0 %copy-start.33 = (pred[72]{0:T(512)(128)(4,1)S(1)}, pred[72]{0:T(512)(128)(4,1)}, u32[]{:S(2)}) copy-start(pred[72]{0:T(512)(128)(4,1)} %copy-done.32) | copy-start | bytes 220
  402.7 13.3 %all-to-all-start.1 = ((bf16[8,16,1152]{2,1,0:T(8,128)(2,1)}), bf16[8,16,1152]{2,1,0:T(8,128)(2,1)S(1)}, u32[]{:S(2)}, u32[]{:S(2)}) async-start(bf16[8,16,1152]{2,1,0:T(8,128)(2,1)} %bitcast.8), calls=%async_computation.1 | async-start | bytes 589824 | tf_op jit(solution)/shard_map/all_to_all | solution.py:403
  417.7 5.0 %collective-permute-start.3 = (bf16[13696]{0:T(1024)(128)(2,1)S(1)}, bf16[13696]{0:T(1024)(128)(2,1)S(1)}, u32[]{:S(2)}, u32[]{:S(2)}) collective-permute-start(bf16[13696]{0:T(1024)(128)(2,1)S(1)} %slice.200), channel_id=1, source_target_pairs={{0,1},{1,2},{2,3},{3,4},{4,5},{5,6},{6,7},{7,8},{8,9},{9,10},{10,1... | collective-permute-start | bytes 82184 | tf_op jit(solution)/shard_map/ppermute | solution.py:412
  425.1 18.5 %all-to-all-start.2 = ((f32[128,1,128]{2,1,0:T(1,128)}), f32[128,1,128]{2,1,0:T(1,128)S(1)}, u32[]{:S(2)}, u32[]{:S(2)}) async-start(f32[128,1,128]{2,1,0:T(1,128)} %broadcast_in_dim.94), calls=%async_computation.2 | async-start | bytes 131072 | tf_op jit(solution)/shard_map/all_to_all | solution.py:418
  436.4 8.6 %copy-start.1 = (f32[82693]{0:T(1024)S(1)}, f32[82693]{0:T(1024)}, u32[]{:S(2)}) copy-start(f32[82693]{0:T(1024)} %param.19) | copy-start | bytes 992320
  436.4 8.6 %copy-start.7 = (f32[82693]{0:T(1024)S(1)}, f32[82693]{0:T(1024)}, u32[]{:S(2)}) copy-start(f32[82693]{0:T(1024)} %param.21) | copy-start | bytes 992320
  436.4 8.6 %copy-start.8 = (f32[82693]{0:T(1024)S(1)}, f32[82693]{0:T(1024)}, u32[]{:S(2)}) copy-start(f32[82693]{0:T(1024)} %param.20) | copy-start | bytes 992320
  (21 other events, 51.7 us)
Sparse Core Ops, SparseCore 0:
  17.7 92.9 all-gather.3
  197.4 29.5 all-gather.5
  279.4 40.3 all-gather.7
  329.6 71.0 reduce-scatter.3

commit v2 on v1

v2 whole, which is shorter than its diff:
```python
import jax
import jax.numpy as jnp
from jax import lax
from jax.experimental import pallas as pl
from jax.experimental.pallas import tpu as pltpu
from jax.sharding import PartitionSpec as P

STEP = 10


LEARN_RATE = 0.03
BETA_ONE = 0.9
BETA_TWO = 0.999
WEIGHT_DECAY = 0.01
EPSILON = 1e-08
CLIP_NORM = 1.0
KEEP_INPUT = 4.0 / 3.0
KEEP_OUTPUT = 4.0 / 3.0
KEEP_RECURRENT = 2.0

LONGEST = 40
LANES = 8
TILE = 8
OWN = TILE + 1
KINDS = 6
PART = 8
UNROLL_FORWARD = 3
UNROLL_BACKWARD = 4
MESSAGE = 88
VMEM_LIMIT = 60 * 2**20

f32 = jnp.float32
bf16 = jnp.bfloat16


def dot(left, right):
    return lax.dot_general(left, right, (((1,), (0,)), ((), ())), preferred_element_type=f32)


def one_hot(rows, columns, wanted):
    row = lax.broadcasted_iota(jnp.int32, (rows, columns), 0)
    column = lax.broadcasted_iota(jnp.int32, (rows, columns), 1)
    return wanted(row, column).astype(bf16)


def place_of(natural, devices):
    owner, rest = natural // OWN, natural % OWN
    return jnp.where(rest < TILE, owner * TILE + rest, devices * TILE + owner)


def step_rows(step):
    return pl.ds(pl.multiple_of(step * LANES, LANES), LANES)


def kept_rows(step, kind):
    return pl.ds(pl.multiple_of((step * KINDS + kind) * LANES, LANES), LANES)


def forward_kernel(
    wall,
    mixed,
    spread,
    collect,
    h_first,
    c_first,
    out_scale,
    hidden_turned,
    output_rows,
    ninth_in,
    kept,
    turned,
    square,
    w_rec,
    ninth,
    apart,
    pre,
    kept_here,
    hiddens,
    outs,
    sems_in,
    sem_ninth,
    sem_rec,
    sems_kept,
    sems_turned,
):
    width = mixed.shape[1]
    main = wall.shape[0]
    devices = main // TILE
    gates_n = 4 * width

    copy_ninth = pltpu.make_async_copy(wall.at[:, pl.ds(2 * gates_n, width)], ninth, sem_ninth)
    copies_in = [
        pltpu.make_async_copy(
            wall.at[:, pl.ds(gate * width, width)],
            square.at[gate, pl.ds(0, main), :],
            sems_in.at[gate],
        )
        for gate in range(4)
    ]
    copy_rec = pltpu.make_async_copy(
        wall.at[:, pl.ds(gates_n, gates_n)], w_rec.at[pl.ds(0, main), :], sem_rec
    )
    copy_ninth.start()
    for copy in copies_in:
        copy.start()
    rows = dot(spread[...], mixed[...]).astype(bf16)
    copy_ninth.wait()
    for tile in range(width // 128):
        columns = pl.ds(tile * 128, 128)
        apart[tile] = ninth[:, columns].astype(f32)
        for gate in range(8):
            rest = apart[tile, pl.ds(gate, devices, stride=8), :].astype(bf16)
            if gate < 4:
                square[gate, pl.ds(main, devices), columns] = rest
                ninth_in[gate, :, columns] = rest
            else:
                there = pl.ds((gate - 4) * width + tile * 128, 128)
                w_rec[pl.ds(main, devices), there] = rest
    copy_rec.start()
    for gate in range(4):
        copies_in[gate].wait()
        pre[:, pl.ds(gate * width, width)] = dot(rows, square[gate])
    copy_rec.wait()
    scale = out_scale[...]

    def step(index, carry):
        hidden, cell = carry
        at = step_rows(index)
        gates = pre[at, :] + dot(hidden.astype(bf16), w_rec[...])
        in_gate = jax.nn.sigmoid(gates[:, :width])
        forget = jax.nn.sigmoid(gates[:, width : 2 * width])
        candid = jnp.tanh(gates[:, 2 * width : 3 * width])
        out_gate = jax.nn.sigmoid(gates[:, 3 * width :])
        cell_new = forget * cell + in_gate * candid
        squash = jnp.tanh(cell_new)
        hidden_new = out_gate * squash
        hiddens[at, :] = hidden
        outs[at, :] = hidden_new * scale
        kept_here[kept_rows(index, 0), :] = out_gate * (1.0 - squash * squash)
        kept_here[kept_rows(index, 1), :] = candid * in_gate * (1.0 - in_gate)
        kept_here[kept_rows(index, 2), :] = cell * forget * (1.0 - forget)
        kept_here[kept_rows(index, 3), :] = in_gate * (1.0 - candid * candid)
        kept_here[kept_rows(index, 4), :] = squash * out_gate * (1.0 - out_gate)
        kept_here[kept_rows(index, 5), :] = forget
        return (hidden_new, cell_new)

    turns = width // 128

    def copy_kept(part):
        size = turns * KINDS * LANES
        at = pl.ds(pl.multiple_of(part * size, LANES), size)
        return pltpu.make_async_copy(kept_here.at[at, :], kept.at[at, :], sems_kept.at[part])

    def copy_turned(gate):
        return pltpu.make_async_copy(square.at[gate], turned.at[gate], sems_turned.at[gate])

    def part(gate, carry):
        def turning(count, carry):
            columns = pl.ds(pl.multiple_of(gate * width + count * 128, 128), 128)
            into = pl.ds(pl.multiple_of(count * 128, 128), 128)
            square[gate, into, :] = w_rec[:, columns].T
            return step(gate * turns + count, carry)

        carry = lax.fori_loop(0, turns, turning, carry, unroll=UNROLL_FORWARD)
        copy_kept(gate).start()
        copy_turned(gate).start()
        return carry

    carry = lax.fori_loop(0, 4, part, (h_first[...], c_first[...]))
    lax.fori_loop(4 * turns, LONGEST, step, carry, unroll=UNROLL_FORWARD)
    begin = 4 * turns * KINDS * LANES
    rest = pl.ds(begin, kept_here.shape[0] - begin)
    last = pltpu.make_async_copy(kept_here.at[rest, :], kept.at[rest, :], sems_kept.at[4])
    last.start()
    hidden_turned[...] = lax.dot_general(
        hiddens[...].astype(bf16),
        collect[...],
        (((0,), (1,)), ((), ())),
        preferred_element_type=f32,
    ).astype(bf16)
    output_rows[...] = dot(collect[...], outs[...].astype(bf16)).astype(bf16)
    for gate in range(4):
        copy_kept(gate).wait()
        copy_turned(gate).wait()
    last.wait()


def backward_kernel(
    turned,
    kept,
    coming,
    spread,
    collect,
    out_scale,
    gate_rows,
    w_turned,
    kept_here,
    come,
    dgates,
    sems_turned,
    sems_kept,
):
    width = coming.shape[1]
    rows = gate_rows.shape[1]
    size = PART * KINDS * LANES
    parts = LONGEST // PART

    def copy_kept(part):
        at = pl.ds(pl.multiple_of(part * size, LANES), size)
        return pltpu.make_async_copy(kept.at[at, :], kept_here.at[at, :], sems_kept.at[part])

    copies = [
        pltpu.make_async_copy(
            turned.at[gate], w_turned.at[pl.ds(gate * width, width), :], sems_turned.at[gate]
        )
        for gate in range(4)
    ]
    copy_kept(parts - 1).start()
    for copy in copies:
        copy.start()
    for part in range(parts - 1):
        copy_kept(parts - 2 - part).start()
    come[...] = dot(spread[...], coming[...])
    scale = out_scale[...]

    def gradients(index, carry):
        dh_next, dc_next = carry
        at = step_rows(index)
        grad_h = come[at, :] * scale + dh_next
        grad_c = dc_next + grad_h * kept_here[kept_rows(index, 0), :]
        grads = jnp.concatenate(
            [
                grad_c * kept_here[kept_rows(index, 1), :],
                grad_c * kept_here[kept_rows(index, 2), :],
                grad_c * kept_here[kept_rows(index, 3), :],
                grad_h * kept_here[kept_rows(index, 4), :],
            ],
            axis=1,
        )
        dgates[at, :] = grads
        return (grads, grad_c * kept_here[kept_rows(index, 5), :])

    def step(index, carry):
        grads, dc_next = gradients(index, carry)
        return (dot(grads.astype(bf16), w_turned[...]), dc_next)

    def run(part, count, carry):
        first = (part + 1) * PART - 1
        return lax.fori_loop(
            0, count, lambda back, c: step(first - back, c), carry, unroll=UNROLL_BACKWARD
        )

    copy_kept(parts - 1).wait()
    for copy in copies:
        copy.wait()
    zero = jnp.zeros((LANES, width), f32)

    def whole_part(back, carry):
        part = parts - 1 - back

        @pl.when(back > 0)
        def _():
            copy_kept(part).wait()

        return run(part, PART, carry)

    carry = lax.fori_loop(0, parts - 1, whole_part, (zero, zero))
    copy_kept(0).wait()
    carry = run(0, PART - 1, carry)
    gradients(0, carry)
    for gate in range(4):
        columns = pl.ds(gate * width, width)
        gate_rows[gate] = dot(
            collect[pl.ds(0, rows), :], dgates[:, columns].astype(bf16)
        ).astype(bf16)


def gradient_kernel(
    core, mixed_all, hidden_all, mine, other, message, left, right, packed, sems_left, sems_right
):
    width = mine.shape[2]
    rows = mine.shape[1]
    half = mine.shape[0]
    line = 2 * half
    slot = mixed_all.shape[1]
    devices = message.shape[0]
    main = devices * TILE
    which = core[0]

    def copies_left(source):
        found = []
        for place in range(line):
            chip, twin = place % half, place // half
            block = 2 * chip + (which if twin == 0 else 1 - which)
            found.append(
                pltpu.make_async_copy(
                    source.at[pl.ds(block * width, width), :],
                    left.at[:, pl.ds(place * slot, slot)],
                    sems_left.at[place],
                )
            )
        return found

    @pl.when(which == 0)
    def _():
        for copy in copies_left(mixed_all):
            copy.start()

    @pl.when(which != 0)
    def _():
        for copy in copies_left(hidden_all):
            copy.start()

    copies_right = [
        pltpu.make_async_copy(
            (mine if place < half else other).at[place % half],
            right.at[pl.ds(place * slot, rows), :],
            sems_right.at[place],
        )
        for place in range(line)
    ]
    for copy in copies_right:
        copy.start()
    for place in range(line):
        right[pl.ds(place * slot + rows, slot - rows), :] = jnp.zeros((slot - rows, width), bf16)
    packed[:, pl.ds(OWN * TILE, TILE * 2), :] = jnp.zeros((devices, TILE * 2, 128), f32)
    for copy in copies_left(mixed_all) + copies_right:
        copy.wait()
    tiles = 3
    for begin in range(0, width // 128, tiles):
        grad = dot(left[...], right[:, pl.ds(begin * 128, tiles * 128)])
        for tile in range(tiles):
            here = grad[:, tile * 128 : (tile + 1) * 128]
            place = begin + tile
            packed[:, pl.ds(place * TILE, TILE), :] = here[:main].reshape(devices, TILE, 128)
            packed[:, OWN * TILE + place, :] = here[main:]
    message[...] = packed[...].astype(bf16)


def settle_kernel(got, to_natural, home, total, placed):
    line = total.shape[0]
    tiles = placed.shape[0]
    half = line // 2
    lines = got.shape[0] // line
    found = got[pl.ds(0, line)].astype(f32)
    for index in range(1, lines):
        found = found + got[pl.ds(index * line, line)].astype(f32)
    total[...] = found
    for source in range(line):
        gate = (source % 2) * half + source // 2
        for tile in range(tiles):
            placed[tile, pl.ds(gate, TILE, stride=8), :] = total[
                source, pl.ds(tile * TILE, TILE), :
            ]
            placed[tile, pl.ds(TILE * 8 + gate, 1), :] = total[
                source, pl.ds(OWN * TILE + tile, 1), :
            ]
    values = jnp.concatenate([placed[tile] for tile in range(tiles)], axis=1)
    high = values.astype(bf16)
    rest = (values - high.astype(f32)).astype(bf16)
    home[...] = dot(high, to_natural[...]) + dot(rest, to_natural[...])


def in_vmem():
    return pl.BlockSpec(memory_space=pltpu.VMEM)


def in_place():
    return pl.BlockSpec(memory_space=pl.ANY)


def run_forward(wall, mixed, spread, collect, h_first, c_first, out_scale):
    steps_rows = spread.shape[0]
    rows, width = mixed.shape
    devices = wall.shape[0] // TILE
    all_kept = LONGEST * KINDS * LANES
    return pl.pallas_call(
        forward_kernel,
        out_shape=(
            jax.ShapeDtypeStruct((width, collect.shape[0]), bf16),
            jax.ShapeDtypeStruct((collect.shape[0], width), bf16),
            jax.ShapeDtypeStruct((4, devices, width), bf16),
            jax.ShapeDtypeStruct((all_kept, width), f32),
            jax.ShapeDtypeStruct((4, width, width), bf16),
        ),
        in_specs=[in_place()] + [in_vmem()] * 6,
        out_specs=(in_vmem(),) * 3 + (in_place(),) * 2,
        scratch_shapes=[
            pltpu.VMEM((4, width, width), bf16),
            pltpu.VMEM((width, 4 * width), bf16),
            pltpu.VMEM((devices * TILE, width), bf16),
            pltpu.VMEM((width // 128, devices * TILE, 128), f32),
            pltpu.VMEM((steps_rows, 4 * width), f32),
            pltpu.VMEM((all_kept, width), f32),
            pltpu.VMEM((steps_rows, width), f32),
            pltpu.VMEM((steps_rows, width), f32),
            pltpu.SemaphoreType.DMA((4,)),
            pltpu.SemaphoreType.DMA,
            pltpu.SemaphoreType.DMA,
            pltpu.SemaphoreType.DMA((5,)),
            pltpu.SemaphoreType.DMA((4,)),
        ],
        compiler_params=pltpu.CompilerParams(vmem_limit_bytes=VMEM_LIMIT),
        cost_estimate=pl.CostEstimate(
            flops=60_000_000_000, bytes_accessed=30_000_000, transcendentals=2_000_000
        ),
        name="forward",
    )(wall, mixed, spread, collect, h_first, c_first, out_scale)


def run_backward(turned, kept, coming, spread, collect, out_scale):
    steps_rows = spread.shape[0]
    rows, width = coming.shape
    return pl.pallas_call(
        backward_kernel,
        out_shape=jax.ShapeDtypeStruct((4, rows, width), bf16),
        in_specs=[in_place()] * 2 + [in_vmem()] * 4,
        out_specs=in_vmem(),
        scratch_shapes=[
            pltpu.VMEM((4 * width, width), bf16),
            pltpu.VMEM(kept.shape, f32),
            pltpu.VMEM((steps_rows, width), f32),
            pltpu.VMEM((steps_rows, 4 * width), f32),
            pltpu.SemaphoreType.DMA((4,)),
            pltpu.SemaphoreType.DMA((LONGEST // PART,)),
        ],
        compiler_params=pltpu.CompilerParams(vmem_limit_bytes=VMEM_LIMIT),
        cost_estimate=pl.CostEstimate(
            flops=60_000_000_000, bytes_accessed=30_000_000, transcendentals=0
        ),
        name="backward",
    )(turned, kept, coming, spread, collect, out_scale)


def run_gradient(core, mixed_all, hidden_all, mine, other, devices):
    half, rows, width = mine.shape
    line, slot = 2 * half, mixed_all.shape[1]
    return pl.pallas_call(
        gradient_kernel,
        out_shape=jax.ShapeDtypeStruct((devices, MESSAGE, 128), bf16),
        in_specs=[pl.BlockSpec(memory_space=pltpu.SMEM)] + [in_place()] * 4,
        out_specs=in_vmem(),
        scratch_shapes=[
            pltpu.VMEM((width, line * slot), bf16),
            pltpu.VMEM((line * slot, width), bf16),
            pltpu.VMEM((devices, MESSAGE, 128), f32),
            pltpu.SemaphoreType.DMA((line,)),
            pltpu.SemaphoreType.DMA((line,)),
        ],
        compiler_params=pltpu.CompilerParams(vmem_limit_bytes=VMEM_LIMIT),
        cost_estimate=pl.CostEstimate(
            flops=6_000_000_000, bytes_accessed=12_000_000, transcendentals=0
        ),
        name="gradient",
    )(core, mixed_all, hidden_all, mine, other)


def run_settle(got, to_natural, line):
    wide, width = to_natural.shape
    return pl.pallas_call(
        settle_kernel,
        out_shape=jax.ShapeDtypeStruct((OWN * 8, width), f32),
        in_specs=[in_vmem()] * 2,
        out_specs=in_vmem(),
        scratch_shapes=[
            pltpu.VMEM((line, MESSAGE, 128), f32),
            pltpu.VMEM((wide // 128, OWN * 8, 128), f32),
        ],
        compiler_params=pltpu.CompilerParams(vmem_limit_bytes=VMEM_LIMIT),
        name="settle",
    )(got, to_natural)


def split_exact(values):
    parts = []
    rest = values
    for _ in range(3):
        part = lax.reduce_precision(rest, 8, 7)
        parts.append(part.astype(bf16))
        rest = rest - part
    return parts


def body(
    inputs,
    d_out,
    h_start,
    c_start,
    pieces,
    in_mask,
    out_mask,
    w_mask,
    master,
    moment_one,
    moment_two,
):
    streams, steps, width = inputs.shape
    gates_n = 4 * width
    count_w = 2 * width * gates_n
    total = count_w + gates_n
    shard = master.shape[0]
    devices = lax.axis_size("batch")
    me = lax.axis_index("batch")
    wide = OWN * devices
    block = OWN * 2 * gates_n
    gap = block - shard
    most = gap * devices
    tokens = streams * steps
    rows_n = -(-tokens // 32) * 32
    slot = -(-tokens // 128) * 128
    line = 8
    lines = devices // line

    line_groups = [[line * q + m for m in range(line)] for q in range(lines)]
    column_groups = [
        [line * q + 2 * y + c for y in range(line // 2)] for q in range(lines) for c in range(2)
    ]
    twins = [(i, i ^ 1) for i in range(devices)]

    to_kept = one_hot(width, wide, lambda k, p: place_of(k, devices) == p)
    to_natural = one_hot(wide, width, lambda p, k: place_of(k, devices) == p)

    places = me * shard + lax.iota(jnp.int32, shard)
    recurrent = (places < count_w) & (places % (2 * gates_n) >= gates_n)
    rec_scale = jnp.where(recurrent, w_mask.astype(f32) * KEEP_RECURRENT, 1.0)
    local_low = master.astype(bf16) * rec_scale.astype(bf16)
    local_low = jnp.where(places < total, local_low, jnp.zeros((), bf16))
    head = lax.ppermute(local_low[:most], "batch", [(i + 1, i) for i in range(devices - 1)])
    own = lax.dynamic_slice(jnp.concatenate([local_low, head]), (gap * me,), (block,))
    own = own.reshape(OWN * 8, width)
    order = one_hot(
        OWN * 8,
        OWN * 8,
        lambda a, b: jnp.where(a < 64, (a % 8) * 8 + a // 8, 64 + a % 8) == b,
    )
    own = dot(order, dot(own, to_kept).astype(bf16)).astype(bf16)
    own = jnp.concatenate([own[TILE * j : TILE * (j + 1)] for j in range(OWN)], axis=1)
    wall = lax.all_gather(own, "batch", axis=0, tiled=True)
    in_scale = in_mask.astype(f32) * KEEP_INPUT
    mixed = (inputs.astype(f32) * in_scale[:, None, :]).astype(bf16).reshape(tokens, width)
    spare = ((0, rows_n - tokens), (0, 0))
    mixed = dot(jnp.pad(mixed, spare), to_kept).astype(bf16)
    bias_place = place_of(jnp.int32(width), devices)
    column = lax.broadcasted_iota(jnp.int32, mixed.shape, 1)
    mixed = jnp.where(column == bias_place, jnp.ones((), bf16), mixed)
    mixed_turned = jnp.pad(mixed, ((0, slot - rows_n), (0, 0))).T
    coming = dot(jnp.pad(d_out.reshape(tokens, width), spare), to_kept).astype(bf16)
    small = jnp.concatenate(
        [h_start.astype(bf16)]
        + split_exact(c_start)
        + [in_mask.astype(bf16), out_mask.astype(bf16)],
        axis=0,
    )
    small = dot(small, to_kept)
    part = [small[streams * j : streams * (j + 1)] for j in range(6)]
    empty = jnp.zeros((LANES - streams, wide), f32)
    h_first = jnp.concatenate([part[0], empty], axis=0)
    c_first = jnp.concatenate([part[1] + part[2] + part[3], empty], axis=0)
    in_scale_kept = part[4] * KEEP_INPUT
    out_scale_kept = part[5] * KEEP_OUTPUT
    out_scale = jnp.concatenate(
        [out_scale_kept, out_scale_kept, jnp.zeros((LANES - 2 * streams, wide), f32)], axis=0
    )
    base = jnp.arange(streams, dtype=jnp.int32) * steps
    none = jnp.zeros((LANES - 2 * streams,), jnp.int32)
    begins = jnp.concatenate([base, base + pieces[:, 0], none])
    lengths = jnp.concatenate([pieces[:, 0], pieces[:, 1], none])
    ticks = lax.broadcasted_iota(jnp.int32, (LONGEST, LANES), 0)
    where = jnp.where(ticks < lengths[None, :], begins[None, :] + ticks, -1).reshape(-1)
    spread = (where[:, None] == lax.iota(jnp.int32, rows_n)[None, :]).astype(bf16)
    collect = (lax.iota(jnp.int32, slot)[:, None] == where[None, :]).astype(bf16)

    mixed_turned, wall = lax.optimization_barrier((mixed_turned, wall))
    mixed_all = lax.all_gather(
        mixed_turned, "batch", axis=0, tiled=True, axis_index_groups=line_groups
    )
    hidden_turned, output_rows, ninth_in, kept, turned = run_forward(
        wall, mixed, spread, collect, h_first, c_first, out_scale
    )
    hidden_all = lax.all_gather(
        hidden_turned, "batch", axis=0, tiled=True, axis_index_groups=line_groups
    )
    gate_rows = run_backward(turned, kept, coming, spread, collect, out_scale)

    mine = lax.all_to_all(
        gate_rows, "batch", 0, 0, tiled=True, axis_index_groups=column_groups
    )
    other = lax.ppermute(mine, "batch", twins)
    core = (me % 2).reshape(1)
    message = run_gradient(core, mixed_all, hidden_all, mine, other, devices)
    got = lax.all_to_all(message, "batch", 0, 0, tiled=True)
    home = run_settle(got, to_natural, line).reshape(block)
    tail = lax.ppermute(home[block - most :], "batch", [(i, i + 1) for i in range(devices - 1)])
    grad_shard = lax.dynamic_slice(
        jnp.concatenate([tail, home]), (most - gap * me,), (shard,)
    )
    grad_shard = grad_shard * rec_scale
    squares = jnp.broadcast_to(jnp.sum(grad_shard * grad_shard), (devices, 128))
    squares = jnp.sum(lax.all_to_all(squares, "batch", 0, 0, tiled=True)[:, 0])
    grad_norm = jnp.sqrt(squares)

    output = dot(output_rows, to_natural)[:tokens].astype(bf16).reshape(streams, steps, width)
    gates_flat = [gate_rows[gate] for gate in range(4)]
    d_main = sum(
        lax.dot_general(
            gates_flat[gate],
            wall[:, gate * wide : (gate + 1) * wide],
            (((1,), (1,)), ((), ())),
            preferred_element_type=f32,
        )
        for gate in range(4)
    )
    d_extra = sum(
        lax.dot_general(
            gates_flat[gate],
            ninth_in[gate],
            (((1,), (1,)), ((), ())),
            preferred_element_type=f32,
        )
        for gate in range(4)
    )
    row_stream = lax.iota(jnp.int32, rows_n) // steps
    d_rows = jnp.concatenate([d_main, d_extra], axis=1)
    stream_scale = sum(
        jnp.where((row_stream == s)[:, None], in_scale_kept[s][None, :], 0.0)
        for s in range(streams)
    )
    d_rows = (d_rows * stream_scale).astype(bf16)
    d_inputs = dot(d_rows, to_natural)[:tokens].astype(bf16).reshape(streams, steps, width)

    factor = jnp.minimum(1.0, CLIP_NORM / (grad_norm + 1e-06))
    clipped = grad_shard * factor
    moment_new = BETA_ONE * moment_one + (1.0 - BETA_ONE) * clipped
    second_new = BETA_TWO * moment_two + (1.0 - BETA_TWO) * clipped * clipped
    first_hat = moment_new / (1.0 - BETA_ONE**STEP)
    second_hat = second_new / (1.0 - BETA_TWO**STEP)
    master_new = master - LEARN_RATE * (
        first_hat / (jnp.sqrt(second_hat) + EPSILON) + WEIGHT_DECAY * master
    )
    return (output, d_inputs, moment_new, second_new, master_new, grad_norm)


def solution(mesh):
    placed = (
        P("batch", None, None),
        P("batch", None, None),
        P("batch", None),
        P("batch", None),
        P("batch", None),
        P("batch", None),
        P("batch", None),
        P("batch"),
        P("batch"),
        P("batch"),
        P("batch"),
    )
    return jax.shard_map(
        body,
        mesh=mesh,
        in_specs=placed,
        out_specs=(
            P("batch", None, None),
            P("batch", None, None),
            P("batch"),
            P("batch"),
            P("batch"),
            P(),
        ),
        check_vma=False,
    )
```

time: 455 us -> 398 us (0.87)
  waiting for transfers between devices: 182 us -> 119 us
  blocking collectives: 0 us -> 29.1 us
  matrix products: 48.3 us -> 26 us
  starting transfers between devices: 30.4 us -> 21.5 us
  Pallas kernels: 153 us -> 158 us
    unnamed x5 -> x3, waiting for transfers between devices: 56.7 us -> 0.05 us
    all_to_all x0 -> x1, blocking collectives: none -> 29.1 us  [body(): lax.all_to_all(gate_rows, 'batch', 0, 0, tiled=True, axis_index_groups=co...]
    all_to_all x2 -> x1, waiting for transfers between devices: 35 us -> 19.5 us  [body(): got = lax.all_to_all(message, 'batch', 0, 0, tiled=True)]
    dot_general x6 -> x4, matrix products: 19.1 us -> 5.65 us  [body(): lax.dot_general(gates_flat[gate], ninth_in[gate], (((1,), (1,)), ((), ())...]
    dot_general x9 -> x6, matrix products: 18.8 us -> 9.09 us  [dot(): lax.dot_general(left, right, (((1,), (0,)), ((), ())), preferred_element_...]
    all_gather x1, waiting for transfers between devices: 83.5 us -> 88.4 us  [body(): wall = lax.all_gather(own, 'batch', axis=0, tiled=True)]
    pallas_call x2 -> x4, Pallas kernels: 153 us -> 158 us  [the longest x1 74 us: run_forward(): pl.pallas_call(forward_kernel, out_shape=(jax.ShapeDtypeStruct((width, co...]
    all_to_all x2 -> x1, starting transfers between devices: 10.5 us -> 6.05 us  [body(): got = lax.all_to_all(message, 'batch', 0, 0, tiled=True)]
  transfers between devices with their start and end apart: 11 -> 8, of which waited for: 7 -> 5; matrix products, arithmetic and copies ran while one was open for 9% -> 10% of each run, Pallas kernels for 17% -> 36%
where the time goes in v2:
time: 398 us; the launch traced here: 393 us
  Pallas kernels  158 us (40%)
  waiting for transfers between devices  119 us (30%)
  blocking collectives  29.1 us (7%)
  matrix products  26 us (7%)
  starting transfers between devices  21.5 us (5%)
  between operations  16.4 us (4%)
  other arithmetic  12.3 us (3%)
  local copies, waits for them, and re-layouts  11 us (3%)
    all_gather x1, waiting for transfers between devices, body(): wall = lax.all_gather(own, 'batch', axis=0, tiled=True)  88.4 us
    pallas_call x1, Pallas kernels, run_forward(): pl.pallas_call(forward_kernel, out_shape=(jax.ShapeDtypeStruct((width, co...  74 us
    pallas_call x1, Pallas kernels, run_backward(): pl.pallas_call(backward_kernel, out_shape=jax.ShapeDtypeStruct((4, rows,...  66 us
    all_to_all x1, blocking collectives, body(): lax.all_to_all(gate_rows, 'batch', 0, 0, tiled=True, axis_index_groups=co...  29.1 us
    all_to_all x1, waiting for transfers between devices, body(): got = lax.all_to_all(message, 'batch', 0, 0, tiled=True)  19.5 us
    pallas_call x1, Pallas kernels, run_gradient(): pl.pallas_call(gradient_kernel, out_shape=jax.ShapeDtypeStruct((devices,...  13.2 us
    dot_general x4, matrix products, body(): lax.dot_general(gates_flat[gate], wall[:, gate * wide:(gate + 1) * wide],...  11.2 us
    dot_general x6, matrix products, dot(): lax.dot_general(left, right, (((1,), (0,)), ((), ())), preferred_element_...  9.09 us
  transfers between devices with their start and end apart: 8, of which 5 were waited for; matrix products, arithmetic and copies ran while one was open for 10% of the time, Pallas kernels for 36%

profile of v2, /device:TPU:1, one launch (start us, length us, event | category | flops | bytes accessed | tf_op | source)
XLA Modules:
  0.0 393.0 jit_solution(13604395488192130160)
XLA Ops:
  8.6 3.3 collective-permute-start
  12.0 1.9 fusion.1
  17.9 1.6 fusion.4
  22.1 88.4 %all-gather.4.cloned.1.call-done.wall = bf16[1024,10368]{1,0:T(8,128)(2,1)} async-done(((bf16[8,10368]{1,0:T(8,128)(2,1)}), bf16[1024,10368]{1,0:T(8,128)(2,1)}) %all-gather.4.cloned.1.call-update) | async-done | bytes 21233680 | tf_op jit(solution)/shard_map/all_gather | solution.py:538
  114.2 1.7 convolution_convert_fusion.1.coming
  117.3 74.0 %forward.1 = (bf16[1152,256]{1,0:T(8,128)(2,1)}, bf16[256,1152]{1,0:T(8,128)(2,1)}, bf16[4,128,1152]{2,1,0:T(8,128)(2,1)}, f32[1920,1152]{1,0:T(8,128)}, bf16[4,1152,1152]{2,1,0:T(8,128)(2,1)}) custom-call(bf16[1024,10368]{1,0:T(8,128)(2,1)} %all-gather.4.cloned.1.call-done.wall, bf16[224,1152]{1,0:T(8,128)(2,1)} %copy.24.mixed, ...), custom_call_target="tpu_custom_call" | custom-call | flops 60000002048 | bytes 30000000 | tf_op jit(solution)/shard_map/forward/pallas_call | solution.py:377
  191.3 66.0 %backward.1 = bf16[4,224,1152]{2,1,0:T(8,128)(2,1)} custom-call(bf16[4,1152,1152]{2,1,0:T(8,128)(2,1)} %get-tuple-element.15.turned, f32[1920,1152]{1,0:T(8,128)} %get-tuple-element.16.kept, bf16[224,1152]{1,0:T(8,128)(2,1)} %convolution_convert_fusion.1.coming, bf16[320,224]{1,0:T(8,128)(2,1)} %fusion.48.spread, bf16[256,320]{1,0:T(8,128)(2,1)} %fusion.35.collect, ...), custom_call_target="tpu_custom_call" | custom-call | flops 60000002048 | bytes 30000000 | tf_op jit(solution)/shard_map/backward/pallas_call | solution.py:414
  257.3 29.1 %all_to_all.19.mine = bf16[4,224,1152]{2,1,0:T(8,128)(2,1)S(1)} all-to-all(bf16[4,224,1152]{2,1,0:T(8,128)(2,1)} %backward.1), channel_id=1, replica_groups={{0,2,4,6},{1,3,5,7},{8,10,12,14},{9,11,13,15},{16,18,20,22},{17,19,21,2..., dimensions={0} | all-to-all | bytes 4128768 | tf_op jit(solution)/shard_map/all_to_all | solution.py:585
  286.5 1.8 collective-permute-start.1
  288.3 3.9 collective-permute-done.1.other
  292.2 13.2 %gradient.1 = bf16[128,88,128]{2,1,0:T(8,128)(2,1)} custom-call(s32[1]{0:T(128)} %bitcast.9.core, bf16[9216,256]{1,0:T(8,128)(2,1)} %all-gather.6.cloned.1.call-done.mixed_all, bf16[9216,256]{1,0:T(8,128)(2,1)} %all-gather.8.cloned.1.call-done.hidden_all, bf16[4,224,1152]{2,1,0:T(8,128)(2,1)} %copy-done.2, bf16[4,224,1152]{2,1,0:T(8,128)(2,1)} %collective-permute-done.1.other), custom_call_target="tpu_custom_call" | custom-call | flops 6000000000 | bytes 12000000 | tf_op jit(solution)/shard_map/gradient/pallas_call | solution.py:438
  305.4 6.1 %all-to-all-start.1 = ((bf16[128,88,128]{2,1,0:T(8,128)(2,1)}), bf16[128,88,128]{2,1,0:T(8,128)(2,1)S(1)}, u32[]{:S(2)}, u32[]{:S(2)}) async-start(bf16[128,88,128]{2,1,0:T(8,128)(2,1)} %gradient.1), calls=%async_computation.1 | async-start | bytes 5767168 | tf_op jit(solution)/shard_map/all_to_all | solution.py:591
  311.4 2.5 fusion.86.to_natural
  319.7 2.6 fusion.5
  322.3 2.6 fusion.7
  324.8 2.6 fusion.9
  327.4 3.5 fusion.19
  330.9 19.5 %all-to-all-done.1.got = bf16[128,88,128]{2,1,0:T(8,128)(2,1)S(1)} async-done(((bf16[128,88,128]{2,1,0:T(8,128)(2,1)}), bf16[128,88,128]{2,1,0:T(8,128)(2,1)S(1)}, u32[]{:S(2)}, u32[]{:S(2)}) %all-to-all-start.1) | async-done | bytes 2883616 | tf_op jit(solution)/shard_map/all_to_all | solution.py:591
  350.4 1.5 copy-done
  352.0 4.7 %settle.1 = f32[72,1150]{1,0:T(8,128)} custom-call(bf16[128,88,128]{2,1,0:T(8,128)(2,1)} %copy-done, bf16[1152,1150]{1,0:T(8,128)(2,1)} %fusion.86.to_natural), custom_call_target="tpu_custom_call" | custom-call | tf_op jit(solution)/shard_map/settle/pallas_call | solution.py:460
  358.0 2.9 collective-permute-start.2
  360.9 2.8 fusion.23
  366.0 7.1 %all-to-all-start.2 = ((f32[128,1,128]{2,1,0:T(1,128)}), f32[128,1,128]{2,1,0:T(1,128)S(1)}, u32[]{:S(2)}, u32[]{:S(2)}) async-start(f32[128,1,128]{2,1,0:T(1,128)} %broadcast_in_dim.94), calls=%async_computation.2 | async-start | bytes 131072 | tf_op jit(solution)/shard_map/all_to_all | solution.py:599
  376.4 6.2 %all-to-all-done.2 = f32[128,1,128]{2,1,0:T(1,128)S(1)} async-done(((f32[128,1,128]{2,1,0:T(1,128)}), f32[128,1,128]{2,1,0:T(1,128)S(1)}, u32[]{:S(2)}, u32[]{:S(2)}) %all-to-all-start.2) | async-done | bytes 65568 | tf_op jit(solution)/shard_map/all_to_all | solution.py:599
  (109 shorter events, 27.1 us)
Async XLA Ops:
  7.2 103.4 %all-gather.4.cloned.1.call-start = ((), (), s32[]{:S(2)}) async-start(), calls=%async_computation.3 | async-start | bytes 21399552 | tf_op jit(solution)/shard_map/all_gather | solution.py:538
  8.6 6.1 %collective-permute-start = (bf16[13696]{0:T(1024)(128)(2,1)S(1)}, bf16[13696]{0:T(1024)(128)(2,1)S(1)}, u32[]{:S(2)}, u32[]{:S(2)}) collective-permute-start(bf16[13696]{0:T(1024)(128)(2,1)S(1)} %slice.152), channel_id=1, source_target_pairs={{1,0},{2,1},{3,2},{4,3},{5,4},{6,5},{7,6},{8,7},{9,8},{10,9},{11,1... | collective-permute-start | bytes 82184 | tf_op jit(solution)/shard_map/ppermute | solution.py:528
  13.9 3.6 copy-start.10
  14.0 3.6 copy-start.5
  17.5 274.7 %all-gather.6.cloned.1.call-start = ((), (), s32[]{:S(2)}) async-start(), calls=%async_computation.4 | async-start | bytes 5308416 | tf_op jit(solution)/shard_map/all_gather | solution.py:574
  17.9 2.7 copy-start.14
  17.9 3.1 copy-start.11
  17.9 3.1 copy-start.12
  17.9 3.1 copy-start.6
  19.5 91.3 %copy-start.13 = (f32[3,1150]{1,0:T(4,128)S(1)}, f32[3,1150]{1,0:T(4,128)}, u32[]{:S(2)}) copy-start(f32[3,1150]{1,0:T(4,128)} %param.14) | copy-start | bytes 41404
  110.6 181.6 %all-gather.8.cloned.1.call-start = ((), (), s32[]{:S(2)}) async-start(), calls=%async_computation.5 | async-start | bytes 5308416 | tf_op jit(solution)/shard_map/all_gather | solution.py:580
  114.2 2.4 copy-start.15
  286.5 5.7 %copy-start.2 = (bf16[4,224,1152]{2,1,0:T(8,128)(2,1)}, bf16[4,224,1152]{2,1,0:T(8,128)(2,1)S(1)}, u32[]{:S(2)}) copy-start(bf16[4,224,1152]{2,1,0:T(8,128)(2,1)S(1)} %all_to_all.19.mine) | copy-start | bytes 6193156
  286.5 5.7 %collective-permute-start.1 = (bf16[4,224,1152]{2,1,0:T(8,128)(2,1)S(1)}, bf16[4,224,1152]{2,1,0:T(8,128)(2,1)}, u32[]{:S(2)}, u32[]{:S(2)}) collective-permute-start(bf16[4,224,1152]{2,1,0:T(8,128)(2,1)S(1)} %all_to_all.19.mine), channel_id=1, source_target_pairs={{0,1},{1,0},{2,3},{3,2},{4,5},{5,4},{6,7},{7,6},{8,9},{9,8},{10,11... | collective-permute-start | bytes 6193160 | tf_op jit(solution)/shard_map/ppermute | solution.py:588
  305.4 45.1 %all-to-all-start.1 = ((bf16[128,88,128]{2,1,0:T(8,128)(2,1)}), bf16[128,88,128]{2,1,0:T(8,128)(2,1)S(1)}, u32[]{:S(2)}, u32[]{:S(2)}) async-start(bf16[128,88,128]{2,1,0:T(8,128)(2,1)} %gradient.1), calls=%async_computation.1 | async-start | bytes 5767168 | tf_op jit(solution)/shard_map/all_to_all | solution.py:591
  313.9 4.5 %copy-start.1 = (bf16[4,224,1152]{2,1,0:T(8,128)(2,1)S(1)}, bf16[4,224,1152]{2,1,0:T(8,128)(2,1)}, u32[]{:S(2)}) copy-start(bf16[4,224,1152]{2,1,0:T(8,128)(2,1)} %backward.1) | copy-start | bytes 6193156
  350.4 1.5 copy-start
  358.0 5.7 %collective-permute-start.2 = (f32[13696]{0:T(1024)S(1)}, f32[13696]{0:T(1024)S(1)}, u32[]{:S(2)}, u32[]{:S(2)}) collective-permute-start(f32[13696]{0:T(1024)S(1)} %slice.177), channel_id=1, source_target_pairs={{0,1},{1,2},{2,3},{3,4},{4,5},{5,6},{6,7},{7,8},{8,9},{9,10},{10,1... | collective-permute-start | bytes 164360 | tf_op jit(solution)/shard_map/ppermute | solution.py:593
  360.9 2.8 copy-start.4
  360.9 12.2 %copy-start.16 = (bf16[256,1152]{1,0:T(8,128)(2,1)S(1)}, bf16[256,1152]{1,0:T(8,128)(2,1)}, u32[]{:S(2)}) copy-start(bf16[256,1152]{1,0:T(8,128)(2,1)} %get-tuple-element.14) | copy-start | bytes 1769476
  366.0 16.6 %all-to-all-start.2 = ((f32[128,1,128]{2,1,0:T(1,128)}), f32[128,1,128]{2,1,0:T(1,128)S(1)}, u32[]{:S(2)}, u32[]{:S(2)}) async-start(f32[128,1,128]{2,1,0:T(1,128)} %broadcast_in_dim.94), calls=%async_computation.2 | async-start | bytes 131072 | tf_op jit(solution)/shard_map/all_to_all | solution.py:599
  374.3 9.6 %copy-start.3 = (f32[82693]{0:T(1024)S(1)}, f32[82693]{0:T(1024)}, u32[]{:S(2)}) copy-start(f32[82693]{0:T(1024)} %param.19) | copy-start | bytes 992320
  374.4 9.6 %copy-start.7 = (f32[82693]{0:T(1024)S(1)}, f32[82693]{0:T(1024)}, u32[]{:S(2)}) copy-start(f32[82693]{0:T(1024)} %param.21) | copy-start | bytes 992320
  374.4 9.6 %copy-start.8 = (f32[82693]{0:T(1024)S(1)}, f32[82693]{0:T(1024)}, u32[]{:S(2)}) copy-start(f32[82693]{0:T(1024)} %param.20) | copy-start | bytes 992320
  (1 other events, 0.7 us)
Sparse Core Ops, SparseCore 0:
  17.6 92.9 all-gather.3
  112.2 33.7 all-gather.5
  191.4 33.2 all-gather.7

commit v3 on v2

--- a/solution.py
+++ b/solution.py
@@ -26,6 +26,7 @@
 PART = 8
 UNROLL_FORWARD = 3
 UNROLL_BACKWARD = 4
+CUT = 640
 MESSAGE = 88
 VMEM_LIMIT = 60 * 2**20
 
@@ -192,7 +193,8 @@
     spread,
     collect,
     out_scale,
-    gate_rows,
+    first_part,
+    second_part,
     w_turned,
     kept_here,
     come,
@@ -201,7 +203,7 @@
     sems_kept,
 ):
     width = coming.shape[1]
-    rows = gate_rows.shape[1]
+    rows, cut = first_part.shape[1:]
     size = PART * KINDS * LANES
     parts = LONGEST // PART
 
@@ -270,21 +272,19 @@
     gradients(0, carry)
     for gate in range(4):
         columns = pl.ds(gate * width, width)
-        gate_rows[gate] = dot(
-            collect[pl.ds(0, rows), :], dgates[:, columns].astype(bf16)
-        ).astype(bf16)
+        natural = dot(collect[pl.ds(0, rows), :], dgates[:, columns].astype(bf16)).astype(bf16)
+        first_part[gate] = natural[:, :cut]
+        second_part[gate] = natural[:, cut:]
 
 
 def gradient_kernel(
-    core, mixed_all, hidden_all, mine, other, message, left, right, packed, sems_left, sems_right
+    core, mixed_all, hidden_all, mine, other, message, left, right, sems_left, sems_right
 ):
-    width = mine.shape[2]
-    rows = mine.shape[1]
-    half = mine.shape[0]
+    half, rows, columns = mine.shape
     line = 2 * half
-    slot = mixed_all.shape[1]
-    devices = message.shape[0]
-    main = devices * TILE
+    lines = message.shape[0]
+    width, slot = left.shape[0], mixed_all.shape[1]
+    main = lines * line * TILE
     which = core[0]
 
     def copies_left(source):
@@ -322,43 +322,101 @@
     for copy in copies_right:
         copy.start()
     for place in range(line):
-        right[pl.ds(place * slot + rows, slot - rows), :] = jnp.zeros((slot - rows, width), bf16)
-    packed[:, pl.ds(OWN * TILE, TILE * 2), :] = jnp.zeros((devices, TILE * 2, 128), f32)
+        right[pl.ds(place * slot + rows, slot - rows), :] = jnp.zeros((slot - rows, columns), bf16)
     for copy in copies_left(mixed_all) + copies_right:
         copy.wait()
-    tiles = 3
-    for begin in range(0, width // 128, tiles):
-        grad = dot(left[...], right[:, pl.ds(begin * 128, tiles * 128)])
-        for tile in range(tiles):
-            here = grad[:, tile * 128 : (tile + 1) * 128]
-            place = begin + tile
-            packed[:, pl.ds(place * TILE, TILE), :] = here[:main].reshape(devices, TILE, 128)
-            packed[:, OWN * TILE + place, :] = here[main:]
-    message[...] = packed[...].astype(bf16)
-
-
-def settle_kernel(got, to_natural, home, total, placed):
-    line = total.shape[0]
+    size = 128
+    for begin in range(0, columns, size):
+        grad = dot(left[...], right[:, pl.ds(begin, size)])
+        packed = jnp.concatenate(
+            [
+                grad[:main].reshape(lines, line * TILE, size),
+                grad[main:].reshape(lines, line, size),
+            ],
+            axis=1,
+        )
+        message[:, :, pl.ds(begin, size)] = packed.astype(bf16)
+
+
+def reduce_kernel(first, second, scale, homeward, squares, packed):
+    line = homeward.shape[0]
+    lines = first.shape[0]
+    total = jnp.zeros((1, 128), f32)
+    packed[:, pl.ds(OWN * TILE, TILE * 2), :] = jnp.zeros((line, TILE * 2, 128), f32)
+    place = 0
+    for source in (first, second):
+        for tile in range(source.shape[2] // 128):
+            columns = pl.ds(tile * 128, 128)
+            found = source[0, :, columns].astype(f32)
+            for index in range(1, lines):
+                found = found + source[index, :, columns].astype(f32)
+            found = found * scale[:, pl.ds(place * 128, 128)].astype(f32)
+            total = total + jnp.sum(found * found, axis=0, keepdims=True)
+            tiles = found[: line * TILE].reshape(line, TILE, 128)
+            packed[:, pl.ds(place * TILE, TILE), :] = tiles
+            packed[:, OWN * TILE + place, :] = found[line * TILE :]
+            place += 1
+    homeward[...] = packed[...].astype(bf16)
+    squares[...] = jnp.broadcast_to(jnp.sum(total, axis=1, keepdims=True), squares.shape)
+
+
+def settle_kernel(got, to_natural, home, placed, wide):
+    line = got.shape[0]
     tiles = placed.shape[0]
     half = line // 2
-    lines = got.shape[0] // line
-    found = got[pl.ds(0, line)].astype(f32)
-    for index in range(1, lines):
-        found = found + got[pl.ds(index * line, line)].astype(f32)
-    total[...] = found
+    wide[...] = got[...].astype(f32)
     for source in range(line):
         gate = (source % 2) * half + source // 2
         for tile in range(tiles):
-            placed[tile, pl.ds(gate, TILE, stride=8), :] = total[
+            placed[tile, pl.ds(gate, TILE, stride=8), :] = wide[
                 source, pl.ds(tile * TILE, TILE), :
             ]
-            placed[tile, pl.ds(TILE * 8 + gate, 1), :] = total[
+            placed[tile, pl.ds(TILE * 8 + gate, 1), :] = wide[
                 source, pl.ds(OWN * TILE + tile, 1), :
             ]
     values = jnp.concatenate([placed[tile] for tile in range(tiles)], axis=1)
-    high = values.astype(bf16)
-    rest = (values - high.astype(f32)).astype(bf16)
-    home[...] = dot(high, to_natural[...]) + dot(rest, to_natural[...])
+    home[...] = dot(values.astype(bf16), to_natural[...]).astype(bf16)
+
+
+def own_kernel(
+    wall, ninth_in, first, second, in_rows, output_rows, to_natural, d_out, out, square, sems
+):
+    width = in_rows.shape[1]
+    rows = in_rows.shape[0]
+    main = wall.shape[0]
+    rest = width - main
+    cut = first.shape[2]
+    copies = []
+    for gate in range(4):
+        copies.append(
+            pltpu.make_async_copy(
+                wall.at[:, pl.ds(gate * width, width)],
+                square.at[gate, pl.ds(0, main), :],
+                sems.at[2 * gate],
+            )
+        )
+        copies.append(
+            pltpu.make_async_copy(
+                ninth_in.at[gate], square.at[gate, pl.ds(main, rest), :], sems.at[2 * gate + 1]
+            )
+        )
+    for copy in copies:
+        copy.start()
+    out[...] = dot(output_rows[pl.ds(0, rows), :], to_natural[...]).astype(bf16)
+
+    def right_product(left, matrix):
+        return lax.dot_general(
+            left, matrix, (((1,), (1,)), ((), ())), preferred_element_type=f32
+        )
+
+    found = jnp.zeros((rows, width), f32)
+    for gate in range(4):
+        copies[2 * gate].wait()
+        copies[2 * gate + 1].wait()
+        found = found + right_product(first[gate], square[gate, :, pl.ds(0, cut)])
+        found = found + right_product(second[gate], square[gate, :, pl.ds(cut, width - cut)])
+    found = found * (in_rows[...].astype(f32) * KEEP_INPUT)
+    d_out[...] = dot(found.astype(bf16), to_natural[...]).astype(bf16)
 
 
 def in_vmem():
@@ -413,9 +471,12 @@
     rows, width = coming.shape
     return pl.pallas_call(
         backward_kernel,
-        out_shape=jax.ShapeDtypeStruct((4, rows, width), bf16),
+        out_shape=(
+            jax.ShapeDtypeStruct((4, rows, CUT), bf16),
+            jax.ShapeDtypeStruct((4, rows, width - CUT), bf16),
+        ),
         in_specs=[in_place()] * 2 + [in_vmem()] * 4,
-        out_specs=in_vmem(),
+        out_specs=(in_vmem(),) * 2,
         scratch_shapes=[
             pltpu.VMEM((4 * width, width), bf16),
             pltpu.VMEM(kept.shape, f32),
@@ -432,18 +493,18 @@
     )(turned, kept, coming, spread, collect, out_scale)
 
 
-def run_gradient(core, mixed_all, hidden_all, mine, other, devices):
-    half, rows, width = mine.shape
+def run_gradient(core, mixed_all, hidden_all, mine, other, lines):
+    half, rows, columns = mine.shape
     line, slot = 2 * half, mixed_all.shape[1]
+    width = mixed_all.shape[0] // line
     return pl.pallas_call(
         gradient_kernel,
-        out_shape=jax.ShapeDtypeStruct((devices, MESSAGE, 128), bf16),
+        out_shape=jax.ShapeDtypeStruct((lines, line * OWN, columns), bf16),
         in_specs=[pl.BlockSpec(memory_space=pltpu.SMEM)] + [in_place()] * 4,
         out_specs=in_vmem(),
         scratch_shapes=[
             pltpu.VMEM((width, line * slot), bf16),
-            pltpu.VMEM((line * slot, width), bf16),
-            pltpu.VMEM((devices, MESSAGE, 128), f32),
+            pltpu.VMEM((line * slot, columns), bf16),
             pltpu.SemaphoreType.DMA((line,)),
             pltpu.SemaphoreType.DMA((line,)),
         ],
@@ -455,20 +516,55 @@
     )(core, mixed_all, hidden_all, mine, other)
 
 
-def run_settle(got, to_natural, line):
+def run_reduce(first, second, scale, line, devices):
+    return pl.pallas_call(
+        reduce_kernel,
+        out_shape=(
+            jax.ShapeDtypeStruct((line, MESSAGE, 128), bf16),
+            jax.ShapeDtypeStruct((devices, 128), f32),
+        ),
+        in_specs=[in_vmem()] * 3,
+        out_specs=(in_vmem(),) * 2,
+        scratch_shapes=[pltpu.VMEM((line, MESSAGE, 128), f32)],
+        compiler_params=pltpu.CompilerParams(vmem_limit_bytes=VMEM_LIMIT),
+        name="reduce",
+    )(first, second, scale)
+
+
+def run_settle(got, to_natural):
     wide, width = to_natural.shape
     return pl.pallas_call(
         settle_kernel,
-        out_shape=jax.ShapeDtypeStruct((OWN * 8, width), f32),
+        out_shape=jax.ShapeDtypeStruct((OWN * 8, width), bf16),
         in_specs=[in_vmem()] * 2,
         out_specs=in_vmem(),
         scratch_shapes=[
-            pltpu.VMEM((line, MESSAGE, 128), f32),
             pltpu.VMEM((wide // 128, OWN * 8, 128), f32),
+            pltpu.VMEM(got.shape, f32),
         ],
         compiler_params=pltpu.CompilerParams(vmem_limit_bytes=VMEM_LIMIT),
         name="settle",
     )(got, to_natural)
+
+
+def run_own(wall, ninth_in, first, second, in_rows, output_rows, to_natural):
+    rows, width = in_rows.shape
+    natural = to_natural.shape[1]
+    return pl.pallas_call(
+        own_kernel,
+        out_shape=(jax.ShapeDtypeStruct((rows, natural), bf16),) * 2,
+        in_specs=[in_place()] * 2 + [in_vmem()] * 5,
+        out_specs=(in_vmem(),) * 2,
+        scratch_shapes=[
+            pltpu.VMEM((4, width, width), bf16),
+            pltpu.SemaphoreType.DMA((8,)),
+        ],
+        compiler_params=pltpu.CompilerParams(vmem_limit_bytes=VMEM_LIMIT),
+        cost_estimate=pl.CostEstimate(
+            flops=8_000_000_000, bytes_accessed=15_000_000, transcendentals=0
+        ),
+        name="own",
+    )(wall, ninth_in, first, second, in_rows, output_rows, to_natural)
 
 
 def split_exact(values):
@@ -512,6 +608,7 @@
     lines = devices // line
 
     line_groups = [[line * q + m for m in range(line)] for q in range(lines)]
+    across_groups = [[line * q + m for q in range(lines)] for m in range(line)]
     column_groups = [
         [line * q + 2 * y + c for y in range(line // 2)] for q in range(lines) for c in range(2)
     ]
@@ -525,17 +622,43 @@
     rec_scale = jnp.where(recurrent, w_mask.astype(f32) * KEEP_RECURRENT, 1.0)
     local_low = master.astype(bf16) * rec_scale.astype(bf16)
     local_low = jnp.where(places < total, local_low, jnp.zeros((), bf16))
-    head = lax.ppermute(local_low[:most], "batch", [(i + 1, i) for i in range(devices - 1)])
-    own = lax.dynamic_slice(jnp.concatenate([local_low, head]), (gap * me,), (block,))
-    own = own.reshape(OWN * 8, width)
+
+    def realigned(flat, following):
+        joined = jnp.concatenate([flat, following])
+        rows = lax.dynamic_slice(joined, (gap * me,), (block,)).reshape(OWN * 8, width)
+        return dot(rows, to_kept).astype(bf16)
+
+    before = [(i + 1, i) for i in range(devices - 1)]
     order = one_hot(
         OWN * 8,
         OWN * 8,
         lambda a, b: jnp.where(a < 64, (a % 8) * 8 + a // 8, 64 + a % 8) == b,
     )
-    own = dot(order, dot(own, to_kept).astype(bf16)).astype(bf16)
+    own = realigned(local_low, lax.ppermute(local_low[:most], "batch", before))
+    own = dot(order, own).astype(bf16)
     own = jnp.concatenate([own[TILE * j : TILE * (j + 1)] for j in range(OWN)], axis=1)
     wall = lax.all_gather(own, "batch", axis=0, tiled=True)
+    room = 16
+    scale_low = rec_scale.astype(bf16)
+    scales = realigned(scale_low, lax.ppermute(scale_low[:most], "batch", before))
+    send = one_hot(
+        line * room,
+        OWN * 8,
+        lambda a, b: (a % room < OWN) & (a % room * 8 + a // room % 2 * 4 + a // room // 2 == b),
+    )
+    scales = lax.all_to_all(
+        dot(send, scales).astype(bf16), "batch", 0, 0, tiled=True, axis_index_groups=line_groups
+    )
+    into = one_hot(
+        line * OWN,
+        line * room,
+        lambda a, b: jnp.where(
+            a < line * TILE, a // TILE * room + a % TILE, a % TILE * room + TILE
+        )
+        == b,
+    )
+    scales = dot(into, scales).astype(bf16)
+
     in_scale = in_mask.astype(f32) * KEEP_INPUT
     mixed = (inputs.astype(f32) * in_scale[:, None, :]).astype(bf16).reshape(tokens, width)
     spare = ((0, rows_n - tokens), (0, 0))
@@ -556,7 +679,10 @@
     empty = jnp.zeros((LANES - streams, wide), f32)
     h_first = jnp.concatenate([part[0], empty], axis=0)
     c_first = jnp.concatenate([part[1] + part[2] + part[3], empty], axis=0)
-    in_scale_kept = part[4] * KEEP_INPUT
+    row_stream = lax.broadcasted_iota(jnp.int32, (rows_n, 1), 0) // steps
+    in_rows = sum(
+        jnp.where(row_stream == s, part[4][s : s + 1], 0.0) for s in range(streams)
+    ).astype(bf16)
     out_scale_kept = part[5] * KEEP_OUTPUT
     out_scale = jnp.concatenate(
         [out_scale_kept, out_scale_kept, jnp.zeros((LANES - 2 * streams, wide), f32)], axis=0
@@ -570,7 +696,10 @@
     spread = (where[:, None] == lax.iota(jnp.int32, rows_n)[None, :]).astype(bf16)
     collect = (lax.iota(jnp.int32, slot)[:, None] == where[None, :]).astype(bf16)
 
-    mixed_turned, wall = lax.optimization_barrier((mixed_turned, wall))
+    ready = (wall, mixed, mixed_turned, coming, spread, collect, h_first, c_first, out_scale)
+    ready = lax.optimization_barrier(ready + (in_rows, to_natural, scales))
+    wall, mixed, mixed_turned, coming, spread, collect, h_first, c_first, out_scale = ready[:9]
+    in_rows, to_natural, scales = ready[9:]
     mixed_all = lax.all_gather(
         mixed_turned, "batch", axis=0, tiled=True, axis_index_groups=line_groups
     )
@@ -582,51 +711,37 @@
     )
     gate_rows = run_backward(turned, kept, coming, spread, collect, out_scale)
 
-    mine = lax.all_to_all(
-        gate_rows, "batch", 0, 0, tiled=True, axis_index_groups=column_groups
-    )
-    other = lax.ppermute(mine, "batch", twins)
     core = (me % 2).reshape(1)
-    message = run_gradient(core, mixed_all, hidden_all, mine, other, devices)
-    got = lax.all_to_all(message, "batch", 0, 0, tiled=True)
-    home = run_settle(got, to_natural, line).reshape(block)
+    mine = [
+        lax.all_to_all(part, "batch", 0, 0, tiled=True, axis_index_groups=column_groups)
+        for part in gate_rows
+    ]
+    other = [lax.ppermute(part, "batch", twins) for part in mine]
+    sums = []
+    for index in range(2):
+        message = run_gradient(core, mixed_all, hidden_all, mine[index], other[index], lines)
+        sums.append(
+            lax.all_to_all(
+                message, "batch", 0, 0, tiled=True, axis_index_groups=across_groups
+            )
+        )
+    homeward, squares = run_reduce(sums[0], sums[1], scales, line, devices)
+    homeward = lax.all_to_all(
+        homeward, "batch", 0, 0, tiled=True, axis_index_groups=line_groups
+    )
+    squares = lax.all_to_all(squares, "batch", 0, 0, tiled=True)
+    home = run_settle(homeward, to_natural).reshape(block)
     tail = lax.ppermute(home[block - most :], "batch", [(i, i + 1) for i in range(devices - 1)])
     grad_shard = lax.dynamic_slice(
         jnp.concatenate([tail, home]), (most - gap * me,), (shard,)
-    )
-    grad_shard = grad_shard * rec_scale
-    squares = jnp.broadcast_to(jnp.sum(grad_shard * grad_shard), (devices, 128))
-    squares = jnp.sum(lax.all_to_all(squares, "batch", 0, 0, tiled=True)[:, 0])
-    grad_norm = jnp.sqrt(squares)
-
-    output = dot(output_rows, to_natural)[:tokens].astype(bf16).reshape(streams, steps, width)
-    gates_flat = [gate_rows[gate] for gate in range(4)]
-    d_main = sum(
-        lax.dot_general(
-            gates_flat[gate],
-            wall[:, gate * wide : (gate + 1) * wide],
-            (((1,), (1,)), ((), ())),
-            preferred_element_type=f32,
-        )
-        for gate in range(4)
-    )
-    d_extra = sum(
-        lax.dot_general(
-            gates_flat[gate],
-            ninth_in[gate],
-            (((1,), (1,)), ((), ())),
-            preferred_element_type=f32,
-        )
-        for gate in range(4)
-    )
-    row_stream = lax.iota(jnp.int32, rows_n) // steps
-    d_rows = jnp.concatenate([d_main, d_extra], axis=1)
-    stream_scale = sum(
-        jnp.where((row_stream == s)[:, None], in_scale_kept[s][None, :], 0.0)
-        for s in range(streams)
-    )
-    d_rows = (d_rows * stream_scale).astype(bf16)
-    d_inputs = dot(d_rows, to_natural)[:tokens].astype(bf16).reshape(streams, steps, width)
+    ).astype(f32)
+    grad_norm = jnp.sqrt(jnp.sum(squares[:, 0]))
+
+    d_rows, out_rows = run_own(
+        wall, ninth_in, gate_rows[0], gate_rows[1], in_rows, output_rows, to_natural
+    )
+    output = out_rows[:tokens].reshape(streams, steps, width)
+    d_inputs = d_rows[:tokens].reshape(streams, steps, width)
 
     factor = jnp.minimum(1.0, CLIP_NORM / (grad_norm + 1e-06))
     clipped = grad_shard * factor

time: 398 us -> 419 us (1.053)
  the two profiles are of different devices: /device:TPU:1 before, /device:TPU:32 now
where the time goes in v3:
time: 419 us; the launch traced here: 411 us
  Pallas kernels  183 us (44%)
  waiting for transfers between devices  79.6 us (19%)
  blocking collectives  63.6 us (15%)
  starting transfers between devices  36.1 us (9%)
  between operations  16.6 us (4%)
  other arithmetic  13.1 us (3%)
  local copies, waits for them, and re-layouts  10.8 us (3%)
  matrix products  7.84 us (2%)
    pallas_call x1, Pallas kernels, run_backward(): pl.pallas_call(backward_kernel, out_shape=(jax.ShapeDtypeStruct((4, rows,...  74 us
    pallas_call x1, Pallas kernels, run_forward(): pl.pallas_call(forward_kernel, out_shape=(jax.ShapeDtypeStruct((width, co...  73.2 us
    all_gather x1, waiting for transfers between devices, body(): wall = lax.all_gather(own, 'batch', axis=0, tiled=True)  55.3 us
    all_to_all x2, blocking collectives, body(): lax.all_to_all(part, 'batch', 0, 0, tiled=True, axis_index_groups=column_...  38.3 us
    all_to_all x1, blocking collectives, body(): lax.all_to_all(message, 'batch', 0, 0, tiled=True, axis_index_groups=acro...  25.3 us
    pallas_call x2, Pallas kernels, run_gradient(): pl.pallas_call(gradient_kernel, out_shape=jax.ShapeDtypeStruct((lines, li...  19.9 us
    pallas_call x1, Pallas kernels, run_own(): pl.pallas_call(own_kernel, out_shape=(jax.ShapeDtypeStruct((rows, natural...  10.2 us
  transfers between devices with their start and end apart: 12, of which 5 were waited for; matrix products, arithmetic and copies ran while one was open for 6% of the time, Pallas kernels for 26%

profile of v3, /device:TPU:32, one launch (start us, length us, event | category | flops | bytes accessed | tf_op | source)
XLA Modules:
  0.0 411.0 jit_solution(3255859430551376883)
XLA Ops:
  8.6 6.1 %collective-permute-start = (bf16[13696]{0:T(1024)(128)(2,1)S(1)}, bf16[13696]{0:T(1024)(128)(2,1)S(1)}, u32[]{:S(2)}, u32[]{:S(2)}) collective-permute-start(bf16[13696]{0:T(1024)(128)(2,1)S(1)} %slice.106), channel_id=1, source_target_pairs={{1,0},{2,1},{3,2},{4,3},{5,4},{6,5},{7,6},{8,7},{9,8},{10,9},{11,1... | collective-permute-start | bytes 82184 | tf_op jit(solution)/shard_map/ppermute | solution.py:637
  14.8 1.9 fusion.1
  19.6 7.4 %collective-permute-start.1 = (bf16[13696]{0:T(1024)(128)(2,1)S(1)}, bf16[13696]{0:T(1024)(128)(2,1)S(1)}, u32[]{:S(2)}, u32[]{:S(2)}) collective-permute-start(bf16[13696]{0:T(1024)(128)(2,1)S(1)} %slice.124), channel_id=1, source_target_pairs={{1,0},{2,1},{3,2},{4,3},{5,4},{6,5},{7,6},{8,7},{9,8},{10,9},{11,1... | collective-permute-start | bytes 82184 | tf_op jit(solution)/shard_map/ppermute | solution.py:643
  35.9 2.4 fusion.4.to_natural
  41.0 3.4 all-to-all-start
  47.0 5.2 %all-to-all-done = bf16[8,16,1152]{2,1,0:T(8,128)(2,1)S(1)} async-done(((bf16[8,16,1152]{2,1,0:T(8,128)(2,1)}), bf16[8,16,1152]{2,1,0:T(8,128)(2,1)S(1)}, u32[]{:S(2)}, u32[]{:S(2)}) %all-to-all-start) | async-done | bytes 294944 | tf_op jit(solution)/shard_map/all_to_all | solution.py:649
  53.2 55.3 %all-gather.4.cloned.1.call-done.wall = bf16[1024,10368]{1,0:T(8,128)(2,1)} async-done(((bf16[8,10368]{1,0:T(8,128)(2,1)}), bf16[1024,10368]{1,0:T(8,128)(2,1)}) %all-gather.4.cloned.1.call-update) | async-done | bytes 21233680 | tf_op jit(solution)/shard_map/all_gather | solution.py:640
  109.5 73.2 %forward.1 = (bf16[1152,256]{1,0:T(8,128)(2,1)}, bf16[256,1152]{1,0:T(8,128)(2,1)}, bf16[4,128,1152]{2,1,0:T(8,128)(2,1)}, f32[1920,1152]{1,0:T(8,128)}, bf16[4,1152,1152]{2,1,0:T(8,128)(2,1)}) custom-call(bf16[1024,10368]{1,0:T(8,128)(2,1)} %all-gather.4.cloned.1.call-done.wall, bf16[224,1152]{1,0:T(8,128)(2,1)} %copy.22.mixed, ...), custom_call_target="tpu_custom_call" | custom-call | flops 60000002048 | bytes 30000000 | tf_op jit(solution)/shard_map/forward/pallas_call | solution.py:435
  183.5 74.0 %backward.1 = (bf16[4,224,640]{2,1,0:T(8,128)(2,1)}, bf16[4,224,512]{2,1,0:T(8,128)(2,1)}) custom-call(bf16[4,1152,1152]{2,1,0:T(8,128)(2,1)} %get-tuple-element.37.turned, f32[1920,1152]{1,0:T(8,128)} %get-tuple-element.38.kept, bf16[224,1152]{1,0:T(8,128)(2,1)} %convolution_convert_fusion.1.coming, bf16[320,224]{1,0:T(8,128)(2,1)} %fusion.19.spread, ...), custom_call_target="tpu_custom_call" | custom-call | flops 60000002048 | bytes 30000000 | tf_op jit(solution)/shard_map/backward/pallas_call | solution.py:472
  257.5 18.8 %all_to_all.49.mine = bf16[4,224,512]{2,1,0:T(8,128)(2,1)S(1)} all-to-all(bf16[4,224,512]{2,1,0:T(8,128)(2,1)} %get-tuple-element.41.second), channel_id=1, replica_groups={{0,2,4,6},{1,3,5,7},{8,10,12,14},{9,11,13,15},{16,18,20,22},{17,19,21,2..., dimensions={0} | all-to-all | bytes 1835008 | tf_op jit(solution)/shard_map/all_to_all | solution.py:716
  276.3 19.5 %all_to_all.50.mine = bf16[4,224,640]{2,1,0:T(8,128)(2,1)S(1)} all-to-all(bf16[4,224,640]{2,1,0:T(8,128)(2,1)S(1)} %copy-done.2), channel_id=1, replica_groups={{0,2,4,6},{1,3,5,7},{8,10,12,14},{9,11,13,15},{16,18,20,22},{17,19,21,2..., dimensions={0} | all-to-all | bytes 2293760 | tf_op jit(solution)/shard_map/all_to_all | solution.py:716
  295.9 9.4 %gradient.3 = bf16[16,72,512]{2,1,0:T(8,128)(2,1)} custom-call(s32[1]{0:T(128)} %bitcast.3.core, bf16[9216,256]{1,0:T(8,128)(2,1)} %all-gather.6.cloned.1.call-done.mixed_all, bf16[9216,256]{1,0:T(8,128)(2,1)} %all-gather.8.cloned.1.call-done.hidden_all, bf16[4,224,512]{2,1,0:T(8,128)(2,1)} %copy-done.4, bf16[4,224,512]{2,1,0:T(8,128)(2,1)} %collective-permute-done.3.other), custom_call_target="tpu_custom_call" | custom-call | flops 6000000000 | bytes 12000000 | tf_op jit(solution)/shard_map/gradient/pallas_call | solution.py:500
  305.3 6.6 %all-to-all-start.4 = ((bf16[16,72,512]{2,1,0:T(8,128)(2,1)}), bf16[16,72,512]{2,1,0:T(8,128)(2,1)S(1)}, u32[]{:S(2)}, u32[]{:S(2)}) async-start(bf16[16,72,512]{2,1,0:T(8,128)(2,1)} %gradient.3), calls=%async_computation.4 | async-start | bytes 2359296 | tf_op jit(solution)/shard_map/all_to_all | solution.py:724
  312.8 10.5 %gradient.2 = bf16[16,72,640]{2,1,0:T(8,128)(2,1)} custom-call(s32[1]{0:T(128)} %bitcast.3.core, bf16[9216,256]{1,0:T(8,128)(2,1)} %all-gather.6.cloned.1.call-done.mixed_all, bf16[9216,256]{1,0:T(8,128)(2,1)} %all-gather.8.cloned.1.call-done.hidden_all, bf16[4,224,640]{2,1,0:T(8,128)(2,1)} %copy-done.3, bf16[4,224,640]{2,1,0:T(8,128)(2,1)} %copy-done.18), custom_call_target="tpu_custom_call" | custom-call | flops 6000000000 | bytes 12000000 | tf_op jit(solution)/shard_map/gradient/pallas_call | solution.py:500
  323.4 5.8 %all-to-all-done.4.second = bf16[16,72,512]{2,1,0:T(8,128)(2,1)S(1)} async-done(((bf16[16,72,512]{2,1,0:T(8,128)(2,1)}), bf16[16,72,512]{2,1,0:T(8,128)(2,1)S(1)}, u32[]{:S(2)}, u32[]{:S(2)}) %all-to-all-start.4) | async-done | bytes 1179680 | tf_op jit(solution)/shard_map/all_to_all | solution.py:724
  329.2 25.3 %all_to_all.51.first = bf16[16,72,640]{2,1,0:T(8,128)(2,1)} all-to-all(bf16[16,72,640]{2,1,0:T(8,128)(2,1)} %gradient.2), channel_id=1, replica_groups={{0,8,16,24,32,40,48,56,64,72,80,88,96,104,112,120},{1,9,17,25,33,41,49,..., dimensions={0} | all-to-all | bytes 2949120 | tf_op jit(solution)/shard_map/all_to_all | solution.py:724
  354.5 2.9 reduce.12
  357.4 3.4 all-to-all-start.5
  360.8 6.6 %all-to-all-done.5.got = bf16[8,88,128]{2,1,0:T(8,128)(2,1)S(1)} async-done(((bf16[8,88,128]{2,1,0:T(8,128)(2,1)}), bf16[8,88,128]{2,1,0:T(8,128)(2,1)S(1)}, u32[]{:S(2)}, u32[]{:S(2)}) %all-to-all-start.5) | async-done | bytes 180256 | tf_op jit(solution)/shard_map/all_to_all | solution.py:729
  367.3 6.8 %all-to-all-start.6 = ((f32[128,1,128]{2,1,0:T(1,128)}), f32[128,1,128]{2,1,0:T(1,128)S(1)}, u32[]{:S(2)}, u32[]{:S(2)}) async-start(f32[128,1,128]{2,1,0:T(1,128)} %bitcast.20), calls=%async_computation.6 | async-start | bytes 131072 | tf_op jit(solution)/shard_map/all_to_all | solution.py:732
  374.1 10.2 %own.1 = (bf16[224,1150]{1,0:T(8,128)(2,1)}, bf16[224,1150]{1,0:T(8,128)(2,1)}) custom-call(bf16[1024,10368]{1,0:T(8,128)(2,1)} %all-gather.4.cloned.1.call-done.wall, bf16[4,128,1152]{2,1,0:T(8,128)(2,1)} %get-tuple-element.36.ninth_in, bf16[4,224,640]{2,1,0:T(8,128)(2,1)} %get-tuple-element.40.first, bf16[4,224,512]{2,1,0:T(8,128)(2,1)} %get-tuple-element.41.second, ...), custom_call_target="tpu_custom_call" | custom-call | flops 8000000000 | bytes 15000000 | tf_op jit(solution)/shard_map/own/pallas_call | solution.py:553
  387.5 3.2 settle.1
  392.0 2.1 collective-permute-start.4
  395.5 6.0 %collective-permute-done.4 = bf16[13696]{0:T(1024)(128)(2,1)S(1)} collective-permute-done((bf16[13696]{0:T(1024)(128)(2,1)S(1)}, bf16[13696]{0:T(1024)(128)(2,1)S(1)}, u32[]{:S(2)}, u32[]{:S(2)}) %collective-permute-start.4) | collective-permute-done | bytes 27424 | tf_op jit(solution)/shard_map/ppermute | solution.py:734
  (123 shorter events, 28.5 us)
Async XLA Ops:
  7.2 101.3 %all-gather.4.cloned.1.call-start = ((), (), s32[]{:S(2)}) async-start(), calls=%async_computation.7 | async-start | bytes 21399552 | tf_op jit(solution)/shard_map/all_gather | solution.py:640
  8.6 8.1 %collective-permute-start = (bf16[13696]{0:T(1024)(128)(2,1)S(1)}, bf16[13696]{0:T(1024)(128)(2,1)S(1)}, u32[]{:S(2)}, u32[]{:S(2)}) collective-permute-start(bf16[13696]{0:T(1024)(128)(2,1)S(1)} %slice.106), channel_id=1, source_target_pairs={{1,0},{2,1},{3,2},{4,3},{5,4},{6,5},{7,6},{8,7},{9,8},{10,9},{11,1... | collective-permute-start | bytes 82184 | tf_op jit(solution)/shard_map/ppermute | solution.py:637
  17.7 9.3 %copy-start.12 = (s32[3,1150]{1,0:T(4,128)S(1)}, s32[3,1150]{1,0:T(4,128)}, u32[]{:S(2)}) copy-start(s32[3,1150]{1,0:T(4,128)} %param.16) | copy-start | bytes 41404
  17.7 9.3 %copy-start.14 = (s32[3,1150]{1,0:T(4,128)S(1)}, s32[3,1150]{1,0:T(4,128)}, u32[]{:S(2)}) copy-start(s32[3,1150]{1,0:T(4,128)} %param.17) | copy-start | bytes 41404
  17.7 9.3 %copy-start.16 = (s32[3,3]{1,0:T(4,128)S(1)}, s32[3,3]{1,0:T(4,128)}, u32[]{:S(2)}) copy-start(s32[3,3]{1,0:T(4,128)} %param.15) | copy-start | bytes 112
  17.7 9.7 %copy-start.6 = (bf16[3,70,1150]{2,1,0:T(8,128)(2,1)S(1)}, bf16[3,70,1150]{2,1,0:T(8,128)(2,1)}, u32[]{:S(2)}) copy-start(bf16[3,70,1150]{2,1,0:T(8,128)(2,1)} %param.11) | copy-start | bytes 1449004
  19.6 18.7 %collective-permute-start.1 = (bf16[13696]{0:T(1024)(128)(2,1)S(1)}, bf16[13696]{0:T(1024)(128)(2,1)S(1)}, u32[]{:S(2)}, u32[]{:S(2)}) collective-permute-start(bf16[13696]{0:T(1024)(128)(2,1)S(1)} %slice.124), channel_id=1, source_target_pairs={{1,0},{2,1},{3,2},{4,3},{5,4},{6,5},{7,6},{8,7},{9,8},{10,9},{11,1... | collective-permute-start | bytes 82184 | tf_op jit(solution)/shard_map/ppermute | solution.py:643
  41.0 11.2 %all-to-all-start = ((bf16[8,16,1152]{2,1,0:T(8,128)(2,1)}), bf16[8,16,1152]{2,1,0:T(8,128)(2,1)S(1)}, u32[]{:S(2)}, u32[]{:S(2)}) async-start(bf16[8,16,1152]{2,1,0:T(8,128)(2,1)} %bitcast.1), calls=%async_computation | async-start | bytes 589824 | tf_op jit(solution)/shard_map/all_to_all | solution.py:649
  44.4 251.4 %all-gather.8.cloned.1.call-start = ((), (), s32[]{:S(2)}) async-start(), calls=%async_computation.9 | async-start | bytes 5308416 | tf_op jit(solution)/shard_map/all_gather | solution.py:709
  182.7 113.1 %all-gather.6.cloned.1.call-start = ((), (), s32[]{:S(2)}) async-start(), calls=%async_computation.8 | async-start | bytes 5308416 | tf_op jit(solution)/shard_map/all_gather | solution.py:703
  257.5 18.8 %copy-start.2 = (bf16[4,224,640]{2,1,0:T(8,128)(2,1)S(1)}, bf16[4,224,640]{2,1,0:T(8,128)(2,1)}, u32[]{:S(2)}) copy-start(bf16[4,224,640]{2,1,0:T(8,128)(2,1)} %get-tuple-element.40.first) | copy-start | bytes 3440644
  276.3 19.6 %copy-start.4 = (bf16[4,224,512]{2,1,0:T(8,128)(2,1)}, bf16[4,224,512]{2,1,0:T(8,128)(2,1)S(1)}, u32[]{:S(2)}) copy-start(bf16[4,224,512]{2,1,0:T(8,128)(2,1)S(1)} %all_to_all.49.mine) | copy-start | bytes 2752516
  276.3 19.5 %collective-permute-start.3 = (bf16[4,224,512]{2,1,0:T(8,128)(2,1)S(1)}, bf16[4,224,512]{2,1,0:T(8,128)(2,1)}, u32[]{:S(2)}, u32[]{:S(2)}) collective-permute-start(bf16[4,224,512]{2,1,0:T(8,128)(2,1)S(1)} %all_to_all.49.mine), channel_id=1, source_target_pairs={{0,1},{1,0},{2,3},{3,2},{4,5},{5,4},{6,7},{7,6},{8,9},{9,8},{10,11... | collective-permute-start | bytes 2752520 | tf_op jit(solution)/shard_map/ppermute | solution.py:719
  295.8 9.5 %copy-start.3 = (bf16[4,224,640]{2,1,0:T(8,128)(2,1)}, bf16[4,224,640]{2,1,0:T(8,128)(2,1)S(1)}, u32[]{:S(2)}) copy-start(bf16[4,224,640]{2,1,0:T(8,128)(2,1)S(1)} %all_to_all.50.mine) | copy-start | bytes 3440644
  295.8 16.1 %collective-permute-start.2 = (bf16[4,224,640]{2,1,0:T(8,128)(2,1)S(1)}, bf16[4,224,640]{2,1,0:T(8,128)(2,1)S(1)}, u32[]{:S(2)}, u32[]{:S(2)}) collective-permute-start(bf16[4,224,640]{2,1,0:T(8,128)(2,1)S(1)} %all_to_all.50.mine), channel_id=1, source_target_pairs={{0,1},{1,0},{2,3},{3,2},{4,5},{5,4},{6,7},{7,6},{8,9},{9,8},{10,11... | collective-permute-start | bytes 3440648 | tf_op jit(solution)/shard_map/ppermute | solution.py:719
  305.3 23.9 %all-to-all-start.4 = ((bf16[16,72,512]{2,1,0:T(8,128)(2,1)}), bf16[16,72,512]{2,1,0:T(8,128)(2,1)S(1)}, u32[]{:S(2)}, u32[]{:S(2)}) async-start(bf16[16,72,512]{2,1,0:T(8,128)(2,1)} %gradient.3), calls=%async_computation.4 | async-start | bytes 2359296 | tf_op jit(solution)/shard_map/all_to_all | solution.py:724
  329.2 25.3 %copy-start = (bf16[16,72,512]{2,1,0:T(8,128)(2,1)}, bf16[16,72,512]{2,1,0:T(8,128)(2,1)S(1)}, u32[]{:S(2)}) copy-start(bf16[16,72,512]{2,1,0:T(8,128)(2,1)S(1)} %all-to-all-done.4.second) | copy-start | bytes 3538948
  357.4 10.0 %all-to-all-start.5 = ((bf16[8,88,128]{2,1,0:T(8,128)(2,1)}), bf16[8,88,128]{2,1,0:T(8,128)(2,1)S(1)}, u32[]{:S(2)}, u32[]{:S(2)}) async-start(bf16[8,88,128]{2,1,0:T(8,128)(2,1)} %get-tuple-element.50), calls=%async_computation.5 | async-start | bytes 360448 | tf_op jit(solution)/shard_map/all_to_all | solution.py:729
  367.3 17.1 %copy-start.5 = (bf16[8,88,128]{2,1,0:T(8,128)(2,1)}, bf16[8,88,128]{2,1,0:T(8,128)(2,1)S(1)}, u32[]{:S(2)}) copy-start(bf16[8,88,128]{2,1,0:T(8,128)(2,1)S(1)} %all-to-all-done.5.got) | copy-start | bytes 540676
  367.3 26.8 %all-to-all-start.6 = ((f32[128,1,128]{2,1,0:T(1,128)}), f32[128,1,128]{2,1,0:T(1,128)S(1)}, u32[]{:S(2)}, u32[]{:S(2)}) async-start(f32[128,1,128]{2,1,0:T(1,128)} %bitcast.20), calls=%async_computation.6 | async-start | bytes 131072 | tf_op jit(solution)/shard_map/all_to_all | solution.py:732
  387.5 13.9 %copy-start.1 = (f32[82693]{0:T(1024)S(1)}, f32[82693]{0:T(1024)}, u32[]{:S(2)}) copy-start(f32[82693]{0:T(1024)} %param.19) | copy-start | bytes 992320
  387.5 13.9 %copy-start.9 = (f32[82693]{0:T(1024)S(1)}, f32[82693]{0:T(1024)}, u32[]{:S(2)}) copy-start(f32[82693]{0:T(1024)} %param.21) | copy-start | bytes 992320
  387.5 13.9 %copy-start.10 = (f32[82693]{0:T(1024)S(1)}, f32[82693]{0:T(1024)}, u32[]{:S(2)}) copy-start(f32[82693]{0:T(1024)} %param.20) | copy-start | bytes 992320
  392.0 9.4 %collective-permute-start.4 = (bf16[13696]{0:T(1024)(128)(2,1)S(1)}, bf16[13696]{0:T(1024)(128)(2,1)S(1)}, u32[]{:S(2)}, u32[]{:S(2)}) collective-permute-start(bf16[13696]{0:T(1024)(128)(2,1)S(1)} %slice.125), channel_id=1, source_target_pairs={{0,1},{1,2},{2,3},{3,4},{4,5},{5,6},{6,7},{7,8},{8,9},{9,10},{10,1... | collective-permute-start | bytes 82184 | tf_op jit(solution)/shard_map/ppermute | solution.py:734
  (7 other events, 25.2 us)
Sparse Core Ops, SparseCore 0:
  19.7 88.7 all-gather.3
  182.9 34.2 all-gather.7
  218.9 34.2 all-gather.5

commit v4 on v3

--- a/solution.py
+++ b/solution.py
@@ -26,8 +26,8 @@
 PART = 8
 UNROLL_FORWARD = 3
 UNROLL_BACKWARD = 4
-CUT = 640
 MESSAGE = 88
+SQUARES = 81
 VMEM_LIMIT = 60 * 2**20
 
 f32 = jnp.float32
@@ -193,8 +193,7 @@
     spread,
     collect,
     out_scale,
-    first_part,
-    second_part,
+    gate_rows,
     w_turned,
     kept_here,
     come,
@@ -203,7 +202,7 @@
     sems_kept,
 ):
     width = coming.shape[1]
-    rows, cut = first_part.shape[1:]
+    rows = gate_rows.shape[1]
     size = PART * KINDS * LANES
     parts = LONGEST // PART
 
@@ -272,9 +271,9 @@
     gradients(0, carry)
     for gate in range(4):
         columns = pl.ds(gate * width, width)
-        natural = dot(collect[pl.ds(0, rows), :], dgates[:, columns].astype(bf16)).astype(bf16)
-        first_part[gate] = natural[:, :cut]
-        second_part[gate] = natural[:, cut:]
+        gate_rows[gate] = dot(
+            collect[pl.ds(0, rows), :], dgates[:, columns].astype(bf16)
+        ).astype(bf16)
 
 
 def gradient_kernel(
@@ -325,46 +324,46 @@
         right[pl.ds(place * slot + rows, slot - rows), :] = jnp.zeros((slot - rows, columns), bf16)
     for copy in copies_left(mixed_all) + copies_right:
         copy.wait()
-    size = 128
-    for begin in range(0, columns, size):
-        grad = dot(left[...], right[:, pl.ds(begin, size)])
-        packed = jnp.concatenate(
-            [
-                grad[:main].reshape(lines, line * TILE, size),
-                grad[main:].reshape(lines, line, size),
-            ],
-            axis=1,
-        )
-        message[:, :, pl.ds(begin, size)] = packed.astype(bf16)
-
-
-def reduce_kernel(first, second, scale, homeward, squares, packed):
+    grad = dot(left[...], right[...])
+    packed = jnp.concatenate(
+        [
+            grad[:main].reshape(lines, line * TILE, columns),
+            grad[main:].reshape(lines, line, columns),
+        ],
+        axis=1,
+    )
+    message[...] = packed.astype(bf16)
+
+
+def reduce_kernel(got, scale, homeward, packed):
     line = homeward.shape[0]
-    lines = first.shape[0]
+    lines = got.shape[0]
+    tiles = got.shape[2] // 128
     total = jnp.zeros((1, 128), f32)
     packed[:, pl.ds(OWN * TILE, TILE * 2), :] = jnp.zeros((line, TILE * 2, 128), f32)
-    place = 0
-    for source in (first, second):
-        for tile in range(source.shape[2] // 128):
-            columns = pl.ds(tile * 128, 128)
-            found = source[0, :, columns].astype(f32)
-            for index in range(1, lines):
-                found = found + source[index, :, columns].astype(f32)
-            found = found * scale[:, pl.ds(place * 128, 128)].astype(f32)
-            total = total + jnp.sum(found * found, axis=0, keepdims=True)
-            tiles = found[: line * TILE].reshape(line, TILE, 128)
-            packed[:, pl.ds(place * TILE, TILE), :] = tiles
-            packed[:, OWN * TILE + place, :] = found[line * TILE :]
-            place += 1
+    for tile in range(tiles):
+        columns = pl.ds(tile * 128, 128)
+        found = got[0, :, columns].astype(f32)
+        for index in range(1, lines):
+            found = found + got[index, :, columns].astype(f32)
+        found = found * scale[:, columns].astype(f32)
+        total = total + jnp.sum(found * found, axis=0, keepdims=True)
+        packed[:, pl.ds(tile * TILE, TILE), :] = found[: line * TILE].reshape(line, TILE, 128)
+        packed[:, OWN * TILE + tile, :] = found[line * TILE :]
+    rest = jnp.broadcast_to(jnp.sum(total, axis=1, keepdims=True), (line, 128))
+    for index in range(3):
+        part = rest.astype(bf16).astype(f32)
+        packed[:, SQUARES + index, :] = part
+        rest = rest - part
     homeward[...] = packed[...].astype(bf16)
-    squares[...] = jnp.broadcast_to(jnp.sum(total, axis=1, keepdims=True), squares.shape)
-
-
-def settle_kernel(got, to_natural, home, placed, wide):
+
+
+def settle_kernel(got, to_natural, home, squares, placed, wide):
     line = got.shape[0]
     tiles = placed.shape[0]
     half = line // 2
     wide[...] = got[...].astype(f32)
+    total = jnp.zeros((1, 128), f32)
     for source in range(line):
         gate = (source % 2) * half + source // 2
         for tile in range(tiles):
@@ -374,18 +373,20 @@
             placed[tile, pl.ds(TILE * 8 + gate, 1), :] = wide[
                 source, pl.ds(OWN * TILE + tile, 1), :
             ]
+        for index in range(3):
+            total = total + wide[source, pl.ds(SQUARES + index, 1), :]
+    squares[...] = jnp.broadcast_to(total, squares.shape)
     values = jnp.concatenate([placed[tile] for tile in range(tiles)], axis=1)
     home[...] = dot(values.astype(bf16), to_natural[...]).astype(bf16)
 
 
 def own_kernel(
-    wall, ninth_in, first, second, in_rows, output_rows, to_natural, d_out, out, square, sems
+    wall, ninth_in, gate_rows, in_rows, output_rows, to_natural, d_out, out, square, sems
 ):
     width = in_rows.shape[1]
     rows = in_rows.shape[0]
     main = wall.shape[0]
     rest = width - main
-    cut = first.shape[2]
     copies = []
     for gate in range(4):
         copies.append(
@@ -413,8 +414,7 @@
     for gate in range(4):
         copies[2 * gate].wait()
         copies[2 * gate + 1].wait()
-        found = found + right_product(first[gate], square[gate, :, pl.ds(0, cut)])
-        found = found + right_product(second[gate], square[gate, :, pl.ds(cut, width - cut)])
+        found = found + right_product(gate_rows[gate], square[gate])
     found = found * (in_rows[...].astype(f32) * KEEP_INPUT)
     d_out[...] = dot(found.astype(bf16), to_natural[...]).astype(bf16)
 
@@ -471,12 +471,9 @@
     rows, width = coming.shape
     return pl.pallas_call(
         backward_kernel,
-        out_shape=(
-            jax.ShapeDtypeStruct((4, rows, CUT), bf16),
-            jax.ShapeDtypeStruct((4, rows, width - CUT), bf16),
-        ),
+        out_shape=jax.ShapeDtypeStruct((4, rows, width), bf16),
         in_specs=[in_place()] * 2 + [in_vmem()] * 4,
-        out_specs=(in_vmem(),) * 2,
+        out_specs=in_vmem(),
         scratch_shapes=[
             pltpu.VMEM((4 * width, width), bf16),
             pltpu.VMEM(kept.shape, f32),
@@ -516,28 +513,28 @@
     )(core, mixed_all, hidden_all, mine, other)
 
 
-def run_reduce(first, second, scale, line, devices):
+def run_reduce(got, scale, line):
     return pl.pallas_call(
         reduce_kernel,
-        out_shape=(
-            jax.ShapeDtypeStruct((line, MESSAGE, 128), bf16),
-            jax.ShapeDtypeStruct((devices, 128), f32),
-        ),
-        in_specs=[in_vmem()] * 3,
-        out_specs=(in_vmem(),) * 2,
+        out_shape=jax.ShapeDtypeStruct((line, MESSAGE, 128), bf16),
+        in_specs=[in_vmem()] * 2,
+        out_specs=in_vmem(),
         scratch_shapes=[pltpu.VMEM((line, MESSAGE, 128), f32)],
         compiler_params=pltpu.CompilerParams(vmem_limit_bytes=VMEM_LIMIT),
         name="reduce",
-    )(first, second, scale)
-
-
-def run_settle(got, to_natural):
+    )(got, scale)
+
+
+def run_settle(got, to_natural, lines):
     wide, width = to_natural.shape
     return pl.pallas_call(
         settle_kernel,
-        out_shape=jax.ShapeDtypeStruct((OWN * 8, width), bf16),
+        out_shape=(
+            jax.ShapeDtypeStruct((OWN * 8, width), bf16),
+            jax.ShapeDtypeStruct((lines, 128), f32),
+        ),
         in_specs=[in_vmem()] * 2,
-        out_specs=in_vmem(),
+        out_specs=(in_vmem(),) * 2,
         scratch_shapes=[
             pltpu.VMEM((wide // 128, OWN * 8, 128), f32),
             pltpu.VMEM(got.shape, f32),
@@ -547,13 +544,13 @@
     )(got, to_natural)
 
 
-def run_own(wall, ninth_in, first, second, in_rows, output_rows, to_natural):
+def run_own(wall, ninth_in, gate_rows, in_rows, output_rows, to_natural):
     rows, width = in_rows.shape
     natural = to_natural.shape[1]
     return pl.pallas_call(
         own_kernel,
         out_shape=(jax.ShapeDtypeStruct((rows, natural), bf16),) * 2,
-        in_specs=[in_place()] * 2 + [in_vmem()] * 5,
+        in_specs=[in_place()] * 2 + [in_vmem()] * 4,
         out_specs=(in_vmem(),) * 2,
         scratch_shapes=[
             pltpu.VMEM((4, width, width), bf16),
@@ -564,7 +561,7 @@
             flops=8_000_000_000, bytes_accessed=15_000_000, transcendentals=0
         ),
         name="own",
-    )(wall, ninth_in, first, second, in_rows, output_rows, to_natural)
+    )(wall, ninth_in, gate_rows, in_rows, output_rows, to_natural)
 
 
 def split_exact(values):
@@ -706,31 +703,29 @@
     hidden_turned, output_rows, ninth_in, kept, turned = run_forward(
         wall, mixed, spread, collect, h_first, c_first, out_scale
     )
+    hidden_turned, mixed_all = lax.optimization_barrier((hidden_turned, mixed_all))
     hidden_all = lax.all_gather(
         hidden_turned, "batch", axis=0, tiled=True, axis_index_groups=line_groups
     )
     gate_rows = run_backward(turned, kept, coming, spread, collect, out_scale)
 
     core = (me % 2).reshape(1)
-    mine = [
-        lax.all_to_all(part, "batch", 0, 0, tiled=True, axis_index_groups=column_groups)
-        for part in gate_rows
-    ]
-    other = [lax.ppermute(part, "batch", twins) for part in mine]
-    sums = []
-    for index in range(2):
-        message = run_gradient(core, mixed_all, hidden_all, mine[index], other[index], lines)
-        sums.append(
-            lax.all_to_all(
-                message, "batch", 0, 0, tiled=True, axis_index_groups=across_groups
-            )
-        )
-    homeward, squares = run_reduce(sums[0], sums[1], scales, line, devices)
+    mine = lax.all_to_all(
+        gate_rows, "batch", 0, 0, tiled=True, axis_index_groups=column_groups
+    )
+    other = lax.ppermute(mine, "batch", twins)
+    message = run_gradient(core, mixed_all, hidden_all, mine, other, lines)
+    got = lax.all_to_all(
+        message, "batch", 0, 0, tiled=True, axis_index_groups=across_groups
+    )
     homeward = lax.all_to_all(
-        homeward, "batch", 0, 0, tiled=True, axis_index_groups=line_groups
-    )
-    squares = lax.all_to_all(squares, "batch", 0, 0, tiled=True)
-    home = run_settle(homeward, to_natural).reshape(block)
+        run_reduce(got, scales, line), "batch", 0, 0, tiled=True, axis_index_groups=line_groups
+    )
+    home, squares = run_settle(homeward, to_natural, lines)
+    squares = lax.all_to_all(
+        squares, "batch", 0, 0, tiled=True, axis_index_groups=across_groups
+    )
+    home = home.reshape(block)
     tail = lax.ppermute(home[block - most :], "batch", [(i, i + 1) for i in range(devices - 1)])
     grad_shard = lax.dynamic_slice(
         jnp.concatenate([tail, home]), (most - gap * me,), (shard,)
@@ -738,7 +733,7 @@
     grad_norm = jnp.sqrt(jnp.sum(squares[:, 0]))
 
     d_rows, out_rows = run_own(
-        wall, ninth_in, gate_rows[0], gate_rows[1], in_rows, output_rows, to_natural
+        wall, ninth_in, gate_rows, in_rows, output_rows, to_natural
     )
     output = out_rows[:tokens].reshape(streams, steps, width)
     d_inputs = d_rows[:tokens].reshape(streams, steps, width)

time: 419 us -> 405 us (0.967)
  the two profiles are of different devices: /device:TPU:32 before, /device:TPU:1 now
where the time goes in v4:
time: 405 us; the launch traced here: 398 us
  Pallas kernels  168 us (41%)
  waiting for transfers between devices  74.6 us (18%)
  blocking collectives  68.8 us (17%)
  starting transfers between devices  35.6 us (9%)
  between operations  16.4 us (4%)
  other arithmetic  15.7 us (4%)
  local copies, waits for them, and re-layouts  11.1 us (3%)
  matrix products  7.87 us (2%)
    pallas_call x1, Pallas kernels, run_forward(): pl.pallas_call(forward_kernel, out_shape=(jax.ShapeDtypeStruct((width, co...  73.2 us
    pallas_call x1, Pallas kernels, run_backward(): pl.pallas_call(backward_kernel, out_shape=jax.ShapeDtypeStruct((4, rows,...  66 us
    all_gather x1, waiting for transfers between devices, body(): wall = lax.all_gather(own, 'batch', axis=0, tiled=True)  59.5 us
    all_to_all x1, blocking collectives, body(): lax.all_to_all(message, 'batch', 0, 0, tiled=True, axis_index_groups=acro...  39.1 us
    all_to_all x1, blocking collectives, body(): lax.all_to_all(gate_rows, 'batch', 0, 0, tiled=True, axis_index_groups=co...  29.7 us
    pallas_call x1, Pallas kernels, run_gradient(): pl.pallas_call(gradient_kernel, out_shape=jax.ShapeDtypeStruct((lines, li...  11.4 us
    pallas_call x1, Pallas kernels, run_own(): pl.pallas_call(own_kernel, out_shape=(jax.ShapeDtypeStruct((rows, natural...  10.9 us
    all_gather x1, starting transfers between devices, body(): lax.all_gather(hidden_turned, 'batch', axis=0, tiled=True, axis_index_gro...  10.7 us
  transfers between devices with their start and end apart: 10, of which 5 were waited for; matrix products, arithmetic and copies ran while one was open for 7% of the time, Pallas kernels for 38%

profile of v4, /device:TPU:1, one launch (start us, length us, event | category | flops | bytes accessed | tf_op | source)
XLA Modules:
  0.0 397.6 jit_solution(4089051041364225725)
XLA Ops:
  8.6 3.3 collective-permute-start
  12.1 1.9 fusion.1
  18.2 1.9 collective-permute-start.1
  25.2 1.8 convolution_convert_fusion.1.coming
  27.0 1.6 fusion.5
  31.1 2.4 fusion.4.to_natural
  34.9 1.8 convolution_convert_fusion.2
  36.7 6.4 %all-to-all-start = ((bf16[8,16,1152]{2,1,0:T(8,128)(2,1)}), bf16[8,16,1152]{2,1,0:T(8,128)(2,1)S(1)}, u32[]{:S(2)}, u32[]{:S(2)}) async-start(bf16[8,16,1152]{2,1,0:T(8,128)(2,1)} %bitcast.1), calls=%async_computation | async-start | bytes 589824 | tf_op jit(solution)/shard_map/all_to_all | solution.py:646
  45.4 4.7 %all-to-all-done = bf16[8,16,1152]{2,1,0:T(8,128)(2,1)S(1)} async-done(((bf16[8,16,1152]{2,1,0:T(8,128)(2,1)}), bf16[8,16,1152]{2,1,0:T(8,128)(2,1)S(1)}, u32[]{:S(2)}, u32[]{:S(2)}) %all-to-all-start) | async-done | bytes 294944 | tf_op jit(solution)/shard_map/all_to_all | solution.py:646
  51.1 59.5 %all-gather.4.cloned.1.call-done.wall = bf16[1024,10368]{1,0:T(8,128)(2,1)} async-done(((bf16[8,10368]{1,0:T(8,128)(2,1)}), bf16[1024,10368]{1,0:T(8,128)(2,1)}) %all-gather.4.cloned.1.call-update) | async-done | bytes 21233680 | tf_op jit(solution)/shard_map/all_gather | solution.py:637
  110.7 10.7 %all-gather.8.cloned.1.call-start = ((), (), s32[]{:S(2)}) async-start(), calls=%async_computation.7 | async-start | bytes 5308416 | tf_op jit(solution)/shard_map/all_gather | solution.py:707
  122.4 73.2 %forward.1 = (bf16[1152,256]{1,0:T(8,128)(2,1)}, bf16[256,1152]{1,0:T(8,128)(2,1)}, bf16[4,128,1152]{2,1,0:T(8,128)(2,1)}, f32[1920,1152]{1,0:T(8,128)}, bf16[4,1152,1152]{2,1,0:T(8,128)(2,1)}) custom-call(bf16[1024,10368]{1,0:T(8,128)(2,1)} %all-gather.4.cloned.1.call-done.wall, bf16[224,1152]{1,0:T(8,128)(2,1)} %copy.22.mixed, ...), custom_call_target="tpu_custom_call" | custom-call | flops 60000002048 | bytes 30000000 | tf_op jit(solution)/shard_map/forward/pallas_call | solution.py:435
  195.6 66.0 %backward.1.gate_rows = bf16[4,224,1152]{2,1,0:T(8,128)(2,1)} custom-call(bf16[4,1152,1152]{2,1,0:T(8,128)(2,1)} %get-tuple-element.37.turned, f32[1920,1152]{1,0:T(8,128)} %get-tuple-element.38.kept, bf16[224,1152]{1,0:T(8,128)(2,1)} %convolution_convert_fusion.1.coming, bf16[320,224]{1,0:T(8,128)(2,1)} %fusion.19.spread, bf16[256,320]{1,0:T(8,128)(2,1)} %fusion.8.collect, ...), custom_call_target="tpu_custom_call" | custom-call | flops 60000002048 | bytes 30000000 | tf_op jit(solution)/shard_map/backward/pallas_call | solution.py:472
  261.7 29.7 %all_to_all.39.mine = bf16[4,224,1152]{2,1,0:T(8,128)(2,1)S(1)} all-to-all(bf16[4,224,1152]{2,1,0:T(8,128)(2,1)} %backward.1.gate_rows), channel_id=1, replica_groups={{0,2,4,6},{1,3,5,7},{8,10,12,14},{9,11,13,15},{16,18,20,22},{17,19,21,2..., dimensions={0} | all-to-all | bytes 4128768 | tf_op jit(solution)/shard_map/all_to_all | solution.py:713
  293.0 3.9 collective-permute-done.2.other
  296.9 11.4 %gradient.1 = bf16[16,72,1152]{2,1,0:T(8,128)(2,1)} custom-call(s32[1]{0:T(128)} %bitcast.3.core, bf16[9216,256]{1,0:T(8,128)(2,1)} %all-gather.6.cloned.1.call-done.mixed_all, bf16[9216,256]{1,0:T(8,128)(2,1)} %all-gather.8.cloned.1.call-done.hidden_all, bf16[4,224,1152]{2,1,0:T(8,128)(2,1)} %copy-done, bf16[4,224,1152]{2,1,0:T(8,128)(2,1)} %collective-permute-done.2.other), custom_call_target="tpu_custom_call" | custom-call | flops 6000000000 | bytes 12000000 | tf_op jit(solution)/shard_map/gradient/pallas_call | solution.py:497
  308.3 39.1 %all_to_all.40.got = bf16[16,72,1152]{2,1,0:T(8,128)(2,1)} all-to-all(bf16[16,72,1152]{2,1,0:T(8,128)(2,1)} %gradient.1), channel_id=1, replica_groups={{0,8,16,24,32,40,48,56,64,72,80,88,96,104,112,120},{1,9,17,25,33,41,49,..., dimensions={0} | all-to-all | bytes 5308416 | tf_op jit(solution)/shard_map/all_to_all | solution.py:718
  347.4 2.9 reduce.12
  350.3 5.1 %all-to-all-start.3 = ((bf16[8,88,128]{2,1,0:T(8,128)(2,1)}), bf16[8,88,128]{2,1,0:T(8,128)(2,1)S(1)}, u32[]{:S(2)}, u32[]{:S(2)}) async-start(bf16[8,88,128]{2,1,0:T(8,128)(2,1)} %reduce.12), calls=%async_computation.3 | async-start | bytes 360448 | tf_op jit(solution)/shard_map/all_to_all | solution.py:721
  355.4 5.8 %all-to-all-done.3.got = bf16[8,88,128]{2,1,0:T(8,128)(2,1)S(1)} async-done(((bf16[8,88,128]{2,1,0:T(8,128)(2,1)}), bf16[8,88,128]{2,1,0:T(8,128)(2,1)S(1)}, u32[]{:S(2)}, u32[]{:S(2)}) %all-to-all-start.3) | async-done | bytes 180256 | tf_op jit(solution)/shard_map/all_to_all | solution.py:721
  361.8 3.1 settle.1
  365.0 3.5 all-to-all-start.4
  368.5 10.9 %own.1 = (bf16[224,1150]{1,0:T(8,128)(2,1)}, bf16[224,1150]{1,0:T(8,128)(2,1)}) custom-call(bf16[1024,10368]{1,0:T(8,128)(2,1)} %all-gather.4.cloned.1.call-done.wall, bf16[4,128,1152]{2,1,0:T(8,128)(2,1)} %get-tuple-element.36.ninth_in, bf16[4,224,1152]{2,1,0:T(8,128)(2,1)} %backward.1.gate_rows, bf16[224,1152]{1,0:T(8,128)(2,1)} %add_convert_fusion.in_rows, ...), custom_call_target="tpu_custom_call" | custom-call | flops 8000000000 | bytes 15000000 | tf_op jit(solution)/shard_map/own/pallas_call | solution.py:550
  383.9 3.0 collective-permute-start.3
  (127 shorter events, 27.7 us)
Async XLA Ops:
  7.2 103.5 %all-gather.4.cloned.1.call-start = ((), (), s32[]{:S(2)}) async-start(), calls=%async_computation.5 | async-start | bytes 21399552 | tf_op jit(solution)/shard_map/all_gather | solution.py:637
  8.6 6.1 %collective-permute-start = (bf16[13696]{0:T(1024)(128)(2,1)S(1)}, bf16[13696]{0:T(1024)(128)(2,1)S(1)}, u32[]{:S(2)}, u32[]{:S(2)}) collective-permute-start(bf16[13696]{0:T(1024)(128)(2,1)S(1)} %slice.106), channel_id=1, source_target_pairs={{1,0},{2,1},{3,2},{4,3},{5,4},{6,5},{7,6},{8,7},{9,8},{10,9},{11,1... | collective-permute-start | bytes 82184 | tf_op jit(solution)/shard_map/ppermute | solution.py:634
  14.0 6.1 %copy-start.9 = (s32[3,1150]{1,0:T(4,128)S(1)}, s32[3,1150]{1,0:T(4,128)}, u32[]{:S(2)}) copy-start(s32[3,1150]{1,0:T(4,128)} %param.16) | copy-start | bytes 41404
  14.0 6.1 %copy-start.3 = (bf16[3,70,1150]{2,1,0:T(8,128)(2,1)S(1)}, bf16[3,70,1150]{2,1,0:T(8,128)(2,1)}, u32[]{:S(2)}) copy-start(bf16[3,70,1150]{2,1,0:T(8,128)(2,1)} %param.11) | copy-start | bytes 1449004
  14.0 6.1 %copy-start.22 = (pred[72]{0:T(512)(128)(4,1)}, pred[72]{0:T(512)(128)(4,1)S(1)}, u32[]{:S(2)}) copy-start(pred[72]{0:T(512)(128)(4,1)S(1)} %iota_compare_fusion.4) | copy-start | bytes 220
  15.6 4.8 %copy-start.4 = (bf16[3,70,1150]{2,1,0:T(8,128)(2,1)S(1)}, bf16[3,70,1150]{2,1,0:T(8,128)(2,1)}, u32[]{:S(2)}) copy-start(bf16[3,70,1150]{2,1,0:T(8,128)(2,1)} %param.12) | copy-start | bytes 1449004
  18.2 15.3 %collective-permute-start.1 = (bf16[13696]{0:T(1024)(128)(2,1)}, bf16[13696]{0:T(1024)(128)(2,1)}, u32[]{:S(2)}, u32[]{:S(2)}) collective-permute-start(bf16[13696]{0:T(1024)(128)(2,1)} %slice.124), channel_id=1, source_target_pairs={{1,0},{2,1},{3,2},{4,3},{5,4},{6,5},{7,6},{8,7},{9,8},{10,9},{11,1... | collective-permute-start | bytes 82184 | tf_op jit(solution)/shard_map/ppermute | solution.py:640
  34.9 15.3 %copy-start.13 = (s32[72]{0:T(128)S(1)}, s32[72]{0:T(128)}, u32[]{:S(2)}) copy-start(s32[72]{0:T(128)} %copy-done.12) | copy-start | bytes 868
  34.9 15.2 %copy-start.15 = (s32[72]{0:T(128)S(1)}, s32[72]{0:T(128)}, u32[]{:S(2)}) copy-start(s32[72]{0:T(128)} %copy-done.14) | copy-start | bytes 868
  34.9 15.2 %copy-start.17 = (s32[72]{0:T(128)S(1)}, s32[72]{0:T(128)}, u32[]{:S(2)}) copy-start(s32[72]{0:T(128)} %copy-done.16) | copy-start | bytes 868
  34.9 15.2 %copy-start.19 = (pred[72]{0:T(512)(128)(4,1)S(1)}, pred[72]{0:T(512)(128)(4,1)}, u32[]{:S(2)}) copy-start(pred[72]{0:T(512)(128)(4,1)} %copy-done.18) | copy-start | bytes 220
  34.9 15.2 %copy-start.21 = (pred[72]{0:T(512)(128)(4,1)S(1)}, pred[72]{0:T(512)(128)(4,1)}, u32[]{:S(2)}) copy-start(pred[72]{0:T(512)(128)(4,1)} %copy-done.20) | copy-start | bytes 220
  34.9 15.2 %copy-start.23 = (pred[72]{0:T(512)(128)(4,1)S(1)}, pred[72]{0:T(512)(128)(4,1)}, u32[]{:S(2)}) copy-start(pred[72]{0:T(512)(128)(4,1)} %copy-done.22) | copy-start | bytes 220
  36.7 13.4 %all-to-all-start = ((bf16[8,16,1152]{2,1,0:T(8,128)(2,1)}), bf16[8,16,1152]{2,1,0:T(8,128)(2,1)S(1)}, u32[]{:S(2)}, u32[]{:S(2)}) async-start(bf16[8,16,1152]{2,1,0:T(8,128)(2,1)} %bitcast.1), calls=%async_computation | async-start | bytes 589824 | tf_op jit(solution)/shard_map/all_to_all | solution.py:646
  43.1 152.5 %all-gather.6.cloned.1.call-start = ((), (), s32[]{:S(2)}) async-start(), calls=%async_computation.6 | async-start | bytes 5308416 | tf_op jit(solution)/shard_map/all_gather | solution.py:700
  110.7 186.2 %all-gather.8.cloned.1.call-start = ((), (), s32[]{:S(2)}) async-start(), calls=%async_computation.7 | async-start | bytes 5308416 | tf_op jit(solution)/shard_map/all_gather | solution.py:707
  291.4 5.5 %copy-start = (bf16[4,224,1152]{2,1,0:T(8,128)(2,1)}, bf16[4,224,1152]{2,1,0:T(8,128)(2,1)S(1)}, u32[]{:S(2)}) copy-start(bf16[4,224,1152]{2,1,0:T(8,128)(2,1)S(1)} %all_to_all.39.mine) | copy-start | bytes 6193156
  291.4 5.5 %collective-permute-start.2 = (bf16[4,224,1152]{2,1,0:T(8,128)(2,1)S(1)}, bf16[4,224,1152]{2,1,0:T(8,128)(2,1)}, u32[]{:S(2)}, u32[]{:S(2)}) collective-permute-start(bf16[4,224,1152]{2,1,0:T(8,128)(2,1)S(1)} %all_to_all.39.mine), channel_id=1, source_target_pairs={{0,1},{1,0},{2,3},{3,2},{4,5},{5,4},{6,7},{7,6},{8,9},{9,8},{10,11... | collective-permute-start | bytes 6193160 | tf_op jit(solution)/shard_map/ppermute | solution.py:716
  350.3 10.9 %all-to-all-start.3 = ((bf16[8,88,128]{2,1,0:T(8,128)(2,1)}), bf16[8,88,128]{2,1,0:T(8,128)(2,1)S(1)}, u32[]{:S(2)}, u32[]{:S(2)}) async-start(bf16[8,88,128]{2,1,0:T(8,128)(2,1)} %reduce.12), calls=%async_computation.3 | async-start | bytes 360448 | tf_op jit(solution)/shard_map/all_to_all | solution.py:721
  365.0 22.0 %all-to-all-start.4 = ((f32[16,1,128]{2,1,0:T(1,128)}), f32[16,1,128]{2,1,0:T(1,128)S(1)}, u32[]{:S(2)}, u32[]{:S(2)}) async-start(f32[16,1,128]{2,1,0:T(1,128)} %bitcast.20), calls=%async_computation.4 | async-start | bytes 16384 | tf_op jit(solution)/shard_map/all_to_all | solution.py:725
  379.3 9.0 %copy-start.1 = (f32[82693]{0:T(1024)S(1)}, f32[82693]{0:T(1024)}, u32[]{:S(2)}) copy-start(f32[82693]{0:T(1024)} %param.19) | copy-start | bytes 992320
  379.4 9.0 %copy-start.5 = (f32[82693]{0:T(1024)S(1)}, f32[82693]{0:T(1024)}, u32[]{:S(2)}) copy-start(f32[82693]{0:T(1024)} %param.21) | copy-start | bytes 992320
  379.4 9.0 %copy-start.6 = (f32[82693]{0:T(1024)S(1)}, f32[82693]{0:T(1024)}, u32[]{:S(2)}) copy-start(f32[82693]{0:T(1024)} %param.20) | copy-start | bytes 992320
  383.9 4.4 %collective-permute-start.3 = (bf16[13696]{0:T(1024)(128)(2,1)S(1)}, bf16[13696]{0:T(1024)(128)(2,1)S(1)}, u32[]{:S(2)}, u32[]{:S(2)}) collective-permute-start(bf16[13696]{0:T(1024)(128)(2,1)S(1)} %slice.125), channel_id=1, source_target_pairs={{0,1},{1,2},{2,3},{3,4},{4,5},{5,6},{6,7},{7,8},{8,9},{9,10},{10,1... | collective-permute-start | bytes 82184 | tf_op jit(solution)/shard_map/ppermute | solution.py:729
  (10 other events, 34.2 us)
Sparse Core Ops, SparseCore 0:
  17.7 92.9 all-gather.3
  112.3 33.7 all-gather.5
  195.8 34.1 all-gather.7
